TPU v7x, 32 devices: a whole 2x2x4 slice. The times are simulated.
32 devices in a mesh: dp: 4 (over y, x), tensor: 8 (over z, core).
Axes of the slice: x: 2, y: 2, z: 4, core: 2. Of those that a mesh axis runs over, the one named last changes fastest.
Arguments:
- features: bfloat16 [1024, 18432], P('tensor', 'dp'), may hold values from -6 to 6
- slot_live: int32 [32], P('dp'), may hold values 0 or 1
- position: float32 [24, 24, 1024], P(None, None, 'tensor'), may hold values from -3 to 3
- gain_outer: float32 [1024], P('tensor'), may hold values from 0.1 to 1.9
- reduce_weight: bfloat16 [1024, 256], P(None, 'tensor'), may hold values from -0.1875 to 0.1875
- gain_middle: float32 [256], P('tensor'), may hold values from 0.1 to 1.9
- conv_weight: bfloat16 [3, 3, 256, 256], P(None, None, None, 'tensor'), may hold values from -0.125 to 0.125
- gain_inner: float32 [256], P('tensor'), may hold values from 0.1 to 1.9
- expand_weight: bfloat16 [256, 1024], P('tensor'), may hold values from -0.5 to 0.5
- readout_weight: bfloat16 [4096, 1024], P('tensor'), may hold values from -0.25 to 0.25
- cotangent: bfloat16 [4096, 4608], P('tensor', 'dp'), may hold values from -6 to 6
Outputs:
- readout: bfloat16 [4096, 4608], P('tensor', 'dp')
- grad_features: float32 [1024, 18432], P('tensor', 'dp')
- grad_position: float32 [24, 24, 1024], P(None, None, 'tensor')
- grad_gain_outer: float32 [1024], P('tensor')
- grad_reduce: float32 [1024, 256], P(None, 'tensor')
- grad_gain_middle: float32 [256], P('tensor')
- grad_conv: float32 [3, 3, 256, 256], P(None, None, None, 'tensor')
- grad_gain_inner: float32 [256], P('tensor')
- grad_expand: float32 [256, 1024], P('tensor')
- grad_readout: float32 [4096, 1024], P('tensor')
All inputs are finite; a program needn't handle non-finite values. No bound on the sum of `slot_live` on one device may be relied on, other than what follows from the above.
Results may differ from a plain program's by a relative error of at most 0.015.
Values may be sent and summed in bfloat16 or wider, within the bound.
A program may use at most 192 MiB of HBM per device.

v0:
```python
import jax
import jax.numpy as jnp
from jax import lax
from jax.sharding import PartitionSpec as P

epsilon = 1e-05


def row_totals(leading, trailing):
    return lax.psum((leading, trailing), "tensor")


def norm_forward(values, norm_gain, breadth):
    totals, squares = row_totals(jnp.sum(values, axis=1), jnp.sum(values * values, axis=1))
    center = totals / breadth
    spread = squares / breadth - center * center
    scaled = lax.rsqrt(spread + epsilon)[:, None]
    normed = (values - center[:, None]) * scaled
    return (normed, scaled, normed * norm_gain)


def norm_backward(grad_out, normed, scaled, norm_gain, breadth):
    grad_normed = grad_out * norm_gain
    gain_grad = jnp.sum(grad_out * normed, axis=0)
    leading, trailing = row_totals(
        jnp.sum(grad_normed, axis=1), jnp.sum(grad_normed * normed, axis=1)
    )
    grad_in = scaled * (
        grad_normed - leading[:, None] / breadth - normed * (trailing[:, None] / breadth)
    )
    return (grad_in, gain_grad)


def silu_grad(inputs):
    gate_value = jax.nn.sigmoid(inputs)
    return gate_value * (1.0 + inputs * (1.0 - gate_value))


def gelu_grad(inputs):
    below = 0.5 * (1.0 + lax.erf(inputs * 0.7071067811865476))
    density = jnp.exp(-0.5 * inputs * inputs) * 0.3989422804014327
    return below + inputs * density


def contract_rows(left_side, right_side):
    return lax.dot_general(
        left_side, right_side, (((0,), (0,)), ((), ())), preferred_element_type=jnp.float32
    )


def window_of(padded, shift_down, shift_across, grid_side):
    images = padded.shape[0]
    breadth = padded.shape[3]
    return padded[
        :, shift_down : shift_down + grid_side, shift_across : shift_across + grid_side, :
    ].reshape(images * grid_side * grid_side, breadth)


def local(
    features,
    slot_live,
    position,
    gain_outer,
    reduce_weight,
    gain_middle,
    conv_weight,
    gain_inner,
    expand_weight,
    readout_weight,
    cotangent,
):
    grid_side = position.shape[0]
    half_side = grid_side // 2
    channel_share = features.shape[0]
    row_count = features.shape[1]
    images = row_count // (grid_side * grid_side)
    tensor_size = lax.axis_size("tensor")
    channels = channel_share * tensor_size
    hidden_share = reduce_weight.shape[1]
    hidden_width = hidden_share * tensor_size
    pooled_count = images * half_side * half_side
    placed = (
        features.T.astype(jnp.float32).reshape(images, grid_side * grid_side, channel_share)
        + position.reshape(1, grid_side * grid_side, channel_share)
    ).reshape(row_count, channel_share)
    live_rows = jnp.repeat(slot_live.astype(jnp.float32), grid_side * grid_side)[:, None]
    normed_outer, scaled_outer, shaped_outer = norm_forward(placed, gain_outer, channels)
    reduce_in = shaped_outer.astype(jnp.bfloat16)
    reduce_full = lax.all_gather(reduce_in, "tensor", axis=1, tiled=True)
    reduced = jnp.dot(reduce_full, reduce_weight, preferred_element_type=jnp.float32)
    normed_middle, scaled_middle, shaped_middle = norm_forward(reduced, gain_middle, hidden_width)
    hidden = jax.nn.silu(shaped_middle).astype(jnp.bfloat16)
    hidden_full = lax.all_gather(hidden, "tensor", axis=1, tiled=True)
    padded_hidden = jnp.pad(
        hidden_full.reshape(images, grid_side, grid_side, hidden_width),
        ((0, 0), (1, 1), (1, 1), (0, 0)),
    )
    convolved = jnp.zeros((row_count, hidden_share), jnp.float32)
    for offset_tap in range(9):
        shift_down = offset_tap // 3
        shift_across = offset_tap % 3
        convolved = convolved + jnp.dot(
            window_of(padded_hidden, shift_down, shift_across, grid_side),
            conv_weight[shift_down, shift_across],
            preferred_element_type=jnp.float32,
        )
    normed_inner, scaled_inner, shaped_inner = norm_forward(convolved, gain_inner, hidden_width)
    activated = jax.nn.silu(shaped_inner).astype(jnp.bfloat16)
    expand_terms = jnp.dot(activated, expand_weight, preferred_element_type=jnp.float32)
    expanded = lax.psum_scatter(expand_terms, "tensor", scatter_dimension=1, tiled=True)
    mixed = placed + live_rows * expanded
    pooled = jnp.mean(mixed.reshape(images, half_side, 2, half_side, 2, channel_share), axis=(2, 4))
    pooled_low = pooled.reshape(pooled_count, channel_share).astype(jnp.bfloat16)
    pooled_full = lax.all_gather(pooled_low, "tensor", axis=1, tiled=True)
    before = lax.dot_general(
        pooled_full, readout_weight, (((1,), (1,)), ((), ())), preferred_element_type=jnp.float32
    )
    readout = jax.nn.gelu(before, approximate=False).astype(jnp.bfloat16).T
    grad_before = (cotangent.T.astype(jnp.float32) * gelu_grad(before)).astype(jnp.bfloat16)
    grad_readout = contract_rows(grad_before, pooled_full)
    pooled_terms = jnp.dot(grad_before, readout_weight, preferred_element_type=jnp.float32)
    grad_pooled = lax.psum_scatter(pooled_terms, "tensor", scatter_dimension=1, tiled=True)
    spread_grad = jnp.broadcast_to(
        (0.25 * grad_pooled).reshape(images, half_side, 1, half_side, 1, channel_share),
        (images, half_side, 2, half_side, 2, channel_share),
    )
    grad_mixed = spread_grad.reshape(row_count, channel_share)
    grad_branch = (live_rows * grad_mixed).astype(jnp.bfloat16)
    grad_full = lax.all_gather(grad_branch, "tensor", axis=1, tiled=True)
    grad_expand = contract_rows(activated, grad_full)
    grad_activated = jnp.dot(grad_full, expand_weight.T, preferred_element_type=jnp.float32)
    grad_convolved, grad_gain_inner = norm_backward(
        grad_activated * silu_grad(shaped_inner),
        normed_inner,
        scaled_inner,
        gain_inner,
        hidden_width,
    )
    grad_conv_low = grad_convolved.astype(jnp.bfloat16)
    tap_grads = []
    grad_padded = jnp.zeros((images, grid_side + 2, grid_side + 2, hidden_width), jnp.float32)
    for offset_tap in range(9):
        shift_down = offset_tap // 3
        shift_across = offset_tap % 3
        tap_grads.append(
            contract_rows(
                window_of(padded_hidden, shift_down, shift_across, grid_side), grad_conv_low
            )
        )
        tap_back = jnp.dot(
            grad_conv_low,
            conv_weight[shift_down, shift_across].T,
            preferred_element_type=jnp.float32,
        )
        grad_padded = grad_padded + jnp.pad(
            tap_back.reshape(images, grid_side, grid_side, hidden_width),
            ((0, 0), (shift_down, 2 - shift_down), (shift_across, 2 - shift_across), (0, 0)),
        )
    grad_conv = jnp.stack(tap_grads, axis=0).reshape(conv_weight.shape)
    grad_window = grad_padded[:, 1 : grid_side + 1, 1 : grid_side + 1, :].reshape(
        row_count, hidden_width
    )
    grad_hidden = lax.psum_scatter(grad_window, "tensor", scatter_dimension=1, tiled=True)
    grad_reduced, grad_gain_middle = norm_backward(
        grad_hidden * silu_grad(shaped_middle),
        normed_middle,
        scaled_middle,
        gain_middle,
        hidden_width,
    )
    grad_reduced_low = grad_reduced.astype(jnp.bfloat16)
    grad_reduce = contract_rows(reduce_full, grad_reduced_low)
    outer_terms = jnp.dot(grad_reduced_low, reduce_weight.T, preferred_element_type=jnp.float32)
    grad_shaped_outer = lax.psum_scatter(outer_terms, "tensor", scatter_dimension=1, tiled=True)
    grad_inputs, grad_gain_outer = norm_backward(
        grad_shaped_outer, normed_outer, scaled_outer, gain_outer, channels
    )
    grad_rows = grad_mixed + grad_inputs
    grad_place = jnp.sum(grad_rows.reshape(images, grid_side, grid_side, channel_share), axis=0)
    grad_total = grad_rows.T
    summed = (
        lax.psum(grad_place.astype(jnp.bfloat16), "dp").astype(jnp.float32),
        lax.psum(grad_gain_outer.astype(jnp.bfloat16), "dp").astype(jnp.float32),
        lax.psum(grad_reduce.astype(jnp.bfloat16), "dp").astype(jnp.float32),
        lax.psum(grad_gain_middle.astype(jnp.bfloat16), "dp").astype(jnp.float32),
        lax.psum(grad_conv.astype(jnp.bfloat16), "dp").astype(jnp.float32),
        lax.psum(grad_gain_inner.astype(jnp.bfloat16), "dp").astype(jnp.float32),
        lax.psum(grad_expand.astype(jnp.bfloat16), "dp").astype(jnp.float32),
        lax.psum(grad_readout.astype(jnp.bfloat16), "dp").astype(jnp.float32),
    )
    return (
        readout,
        grad_total,
        summed[0],
        summed[1],
        summed[2],
        summed[3],
        summed[4],
        summed[5],
        summed[6],
        summed[7],
    )


def solution(mesh):
    return jax.shard_map(
        local,
        mesh=mesh,
        in_specs=(
            P("tensor", "dp"),
            P("dp"),
            P(None, None, "tensor"),
            P("tensor"),
            P(None, "tensor"),
            P("tensor"),
            P(None, None, None, "tensor"),
            P("tensor"),
            P("tensor", None),
            P("tensor", None),
            P("tensor", "dp"),
        ),
        out_specs=(
            P("tensor", "dp"),
            P("tensor", "dp"),
            P(None, None, "tensor"),
            P("tensor"),
            P(None, "tensor"),
            P("tensor"),
            P(None, None, None, "tensor"),
            P("tensor"),
            P("tensor", None),
            P("tensor", None),
        ),
        check_vma=False,
    )
```

profile of v0, /device:TPU:0, one launch (start us, length us, event | category | flops | bytes accessed | tf_op | source)
XLA Modules:
  0.0 1112.5 jit_solution(16768051681533236495)
XLA Ops:
  10.4 30.8 %all-reduce.15 = (f32[4608]{0:T(1024)S(1)}, f32[4608]{0:T(1024)S(1)}) all-reduce(f32[4608]{0:T(1024)S(1)} %get-tuple-element.34, f32[4608]{0:T(1024)S(1)} %get-tuple-element.33), channel_id=1, replica_groups=mesh['dp'=4,'tensor'=8] {'tensor'}, use_global_device_ids=true, to_apply=%region_3.0 | all-reduce | flops 9216 | bytes 73728 | tf_op jit(solution)/shard_map/psum | solution.py:10
  43.6 89.5 %all-gather.5.cloned.1.call-done = bf16[4608,1024]{1,0:T(8,128)(2,1)} async-done(((bf16[4608,128]{1,0:T(8,128)(2,1)}), bf16[4608,1024]{1,0:T(8,128)(2,1)}) %all-gather.5.cloned.1.call-update) | async-done | bytes 9437200 | tf_op jit(solution)/shard_map/all_gather | solution.py:89
  133.1 6.6 fusion.110
  139.7 27.3 %all-reduce.14 = (f32[4608]{0:T(1024)S(1)}, f32[4608]{0:T(1024)S(1)}) all-reduce(f32[4608]{0:T(1024)S(1)} %get-tuple-element.44, f32[4608]{0:T(1024)S(1)} %get-tuple-element.43), channel_id=1, replica_groups=mesh['dp'=4,'tensor'=8] {'tensor'}, use_global_device_ids=true, to_apply=%region_7.0 | all-reduce | flops 9216 | bytes 73728 | tf_op jit(solution)/shard_map/psum | solution.py:10
  168.6 28.6 %all-gather.7.cloned.1.call-done = bf16[4608,256]{0,1:T(8,128)(2,1)} async-done(((bf16[4608,32]{0,1:T(8,128)(2,1)}), bf16[4608,256]{0,1:T(8,128)(2,1)}) %all-gather.7.cloned.1.call-update) | async-done | bytes 2359312 | tf_op jit(solution)/shard_map/all_gather | solution.py:93
  197.2 4.3 copy.36
  201.5 11.9 %pad_slice_fusion = (bf16[8,24,24,256]{3,2,1,0:T(8,128)(2,1)S(1)}, bf16[8,24,24,256]{3,2,1,0:T(8,128)(2,1)S(1)}, bf16[8,24,24,256]{3,2,1,0:T(8,128)(2,1)S(1)}, b...) fusion(bf16[8,24,24,256]{3,2,1,0:T(8,128)(2,1)} %bitcast.357), kind=kLoop, calls=%fused_computation.16 | loop fusion | bytes 21233664 | tf_op jit(solution)/shard_map/slice | solution.py:54
  223.1 27.6 %all-reduce.13 = (f32[4608]{0:T(1024)S(1)}, f32[4608]{0:T(1024)S(1)}) all-reduce(f32[4608]{0:T(1024)S(1)} %get-tuple-element.42, f32[4608]{0:T(1024)S(1)} %get-tuple-element.41), channel_id=1, replica_groups=mesh['dp'=4,'tensor'=8] {'tensor'}, use_global_device_ids=true, to_apply=%region_11.12 | all-reduce | flops 9216 | bytes 73728 | tf_op jit(solution)/shard_map/psum | solution.py:10
  250.8 8.0 fusion.108
  259.6 185.4 %reduce-scatter.5.cloned.1.call-done = f32[4608,128]{1,0:T(8,128)} async-done(((f32[4608,1024]{1,0:T(8,128)}), f32[4608,128]{1,0:T(8,128)}) %reduce-scatter.5.cloned.1.call-update) | async-done | bytes 2359312 | tf_op jit(solution)/shard_map/reduce_scatter | solution.py:110
  445.0 3.7 fusion.12
  448.8 4.4 reduce_sum.159
  457.7 28.7 %all-gather.9.cloned.1.call-done = bf16[1152,1024]{1,0:T(8,128)(2,1)} async-done(((bf16[1152,128]{1,0:T(8,128)(2,1)}), bf16[1152,1024]{1,0:T(8,128)(2,1)}) %all-gather.9.cloned.1.call-update) | async-done | bytes 2359312 | tf_op jit(solution)/shard_map/all_gather | solution.py:114
  486.5 8.5 fusion.4
  497.1 3.6 fusion.111
  500.7 53.8 %reduce-scatter.7.cloned.1.call-done = f32[1152,128]{1,0:T(8,128)} async-done(((f32[1152,1024]{1,0:T(8,128)}), f32[1152,128]{1,0:T(8,128)}) %reduce-scatter.7.cloned.1.call-update) | async-done | bytes 589840 | tf_op jit(solution)/shard_map/reduce_scatter | solution.py:122
  560.6 89.6 %all-gather.11.cloned.1.call-done = bf16[4608,1024]{1,0:T(8,128)(2,1)} async-done(((bf16[4608,128]{1,0:T(8,128)(2,1)}), bf16[4608,1024]{1,0:T(8,128)(2,1)}) %all-gather.11.cloned.1.call-update) | async-done | bytes 9437200 | tf_op jit(solution)/shard_map/all_gather | solution.py:129
  650.2 6.8 multiply_reduce_fusion.1
  657.0 27.8 %all-reduce.12 = (f32[4608]{0:T(1024)S(1)}, f32[4608]{0:T(1024)S(1)}) all-reduce(f32[4608]{0:T(1024)S(1)} %get-tuple-element.36, f32[4608]{0:T(1024)S(1)} %get-tuple-element.40), channel_id=1, replica_groups=mesh['dp'=4,'tensor'=8] {'tensor'}, use_global_device_ids=true, to_apply=%region_18.19 | all-reduce | flops 9216 | bytes 73728 | tf_op jit(solution)/shard_map/psum | solution.py:10
  707.5 11.7 %pad_add_fusion.1 = f32[8,24,24,256]{3,2,1,0:T(8,128)} fusion(f32[8,24,24,256]{3,2,1,0:T(8,128)S(1)} %bitcast.355, f32[8,24,24,256]{3,2,1,0:T(8,128)} %fusion.62, f32[8,24,24,256]{3,2,1,0:T(8,128)} %fusion.64, f32[8,24,24,256]{3,2,1,0:T(8,128)} %fusion.66, f32[8,24,24,256]{3,2,1,0:T(8,128)} %fusion.68, f32[8,24,24,256]{3,2,1,0:T(8,128)} %fusion.70, ...), kind=kLoop, calls=%fused_computation.10 | loop fusion | flops 7077888 | bytes 37748736 | tf_op jit(solution)/shard_map/add | solution.py:155
  719.2 6.0 copy.47
  725.3 52.4 %reduce-scatter.9.cloned.1.call-done = f32[4608,32]{0,1:T(8,128)} async-done(((f32[4608,256]{0,1:T(8,128)}), f32[4608,32]{0,1:T(8,128)}) %reduce-scatter.9.cloned.1.call-update) | async-done | bytes 589840 | tf_op jit(solution)/shard_map/reduce_scatter | solution.py:163
  779.4 26.6 %all-reduce.11 = (f32[4608]{0:T(1024)S(1)}, f32[4608]{0:T(1024)S(1)}) all-reduce(f32[4608]{0:T(1024)S(1)} %get-tuple-element.38, f32[4608]{0:T(1024)S(1)} %get-tuple-element.39), channel_id=1, replica_groups=mesh['dp'=4,'tensor'=8] {'tensor'}, use_global_device_ids=true, to_apply=%region_23.24 | all-reduce | flops 9216 | bytes 73728 | tf_op jit(solution)/shard_map/psum | solution.py:10
  807.0 7.9 fusion.112
  816.1 4.3 convolution_convert_fusion
  837.2 164.0 %reduce-scatter.11.cloned.1.call-done = f32[4608,128]{1,0:T(8,128)} async-done(((f32[4608,1024]{1,0:T(8,128)}), f32[4608,128]{1,0:T(8,128)}) %reduce-scatter.11.cloned.1.call-update) | async-done | bytes 2359312 | tf_op jit(solution)/shard_map/reduce_scatter | solution.py:174
  1001.2 4.3 fusion.26
  1005.5 26.7 %all-reduce.10 = (f32[4608]{0:T(1024)S(1)}, f32[4608]{0:T(1024)S(1)}) all-reduce(f32[4608]{0:T(1024)S(1)} %get-tuple-element.31, f32[4608]{0:T(1024)S(1)} %get-tuple-element.32), channel_id=1, replica_groups=mesh['dp'=4,'tensor'=8] {'tensor'}, use_global_device_ids=true, to_apply=%region_28.29 | all-reduce | flops 9216 | bytes 73728 | tf_op jit(solution)/shard_map/psum | solution.py:10
  1032.2 6.3 fusion.25
  1042.5 10.1 all-reduce.16
  1054.2 3.2 copy.49
  1057.3 42.5 %all-reduce.20.cloned.1.call-done = (bf16[24,24,128]{2,1,0:T(8,128)(2,1)}, bf16[1024,32]{0,1:T(8,128)(2,1)}, bf16[3,3,256,32]{2,3,1,0:T(8,128)(2,1)}, bf16[32,1024]{1,0:T(8,128)(2,1)}, bf16[512,1024]{1,0:T(8,128)(2,1)}) async-done(((bf16[24,24,128]{2,1,0:T(8,128)(2,1)}, bf16[1024,32]{0,1:T(8,128)(2,1)}, bf16[3,3,256,32]{2,3,1,0:T(8,128)(2,1)}, bf16[32,1024]{1,0:T(8,128)(2,1)}, bf16[512,1024]{1,0:T(8,128)(2,1)}), ...) | async-done | bytes 1474576 | tf_op jit(solution)/shard_map/psum | solution.py:182
  (198 shorter events, 84.7 us)
Async XLA Ops:
  7.2 479.3 %copy-start = (bf16[512,1024]{1,0:T(8,128)(2,1)S(1)}, bf16[512,1024]{1,0:T(8,128)(2,1)}, u32[]{:S(2)}) copy-start(bf16[512,1024]{1,0:T(8,128)(2,1)} %param.20) | copy-start | bytes 3145732
  7.2 34.0 %copy-start.44 = (f32[128]{0:T(128)S(1)}, f32[128]{0:T(128)}, u32[]{:S(2)}) copy-start(f32[128]{0:T(128)} %param.14) | copy-start | bytes 1540
  7.2 125.8 %all-gather.5.cloned.1.call-start = ((), (), s32[]{:S(2)}) async-start(), calls=%async_computation.4 | async-start | bytes 10616832 | tf_op jit(solution)/shard_map/all_gather | solution.py:89
  10.4 122.7 %copy-start.32 = (bf16[1024,32]{0,1:T(8,128)(2,1)S(1)}, bf16[1024,32]{0,1:T(8,128)(2,1)}, u32[]{:S(2)}) copy-start(bf16[1024,32]{0,1:T(8,128)(2,1)} %param.15) | copy-start | bytes 196612
  43.5 123.6 %copy-start.42 = (f32[32]{0:T(128)S(1)}, f32[32]{0:T(128)}, u32[]{:S(2)}) copy-start(f32[32]{0:T(128)} %param.16) | copy-start | bytes 388
  43.5 153.7 %all-gather.7.cloned.1.call-start = ((), (), s32[]{:S(2)}) async-start(), calls=%async_computation.5 | async-start | bytes 2654208 | tf_op jit(solution)/shard_map/all_gather | solution.py:93
  139.7 61.7 %copy-start.20 = (f32[4608,32]{0,1:T(8,128)}, f32[4608,32]{0,1:T(8,128)S(1)}, u32[]{:S(2)}) copy-start(f32[4608,32]{0,1:T(8,128)S(1)} %get-tuple-element.80) | copy-start | bytes 1769476
  168.1 276.9 %reduce-scatter.5.cloned.1.call-start = ((), (), s32[]{:S(2)}) async-start(), calls=%async_computation.6 | async-start | bytes 21233664 | tf_op jit(solution)/shard_map/reduce_scatter | solution.py:110
  201.5 12.0 %copy-start.30 = (bf16[3,3,256,32]{2,3,1,0:T(8,128)(2,1)S(1)}, bf16[3,3,256,32]{2,3,1,0:T(8,128)(2,1)}, u32[]{:S(2)}) copy-start(bf16[3,3,256,32]{2,3,1,0:T(8,128)(2,1)} %param.17) | copy-start | bytes 442372
  213.4 8.9 copy-start.4
  222.2 28.5 %copy-start.37 = (bf16[32,1024]{1,0:T(8,128)(2,1)S(1)}, bf16[32,1024]{1,0:T(8,128)(2,1)}, u32[]{:S(2)}) copy-start(bf16[32,1024]{1,0:T(8,128)(2,1)} %param.19) | copy-start | bytes 196612
  222.3 28.5 %copy-start.41 = (f32[32]{0:T(128)S(1)}, f32[32]{0:T(128)}, u32[]{:S(2)}) copy-start(f32[32]{0:T(128)} %param.18) | copy-start | bytes 388
  223.1 461.6 %copy-start.18 = (f32[4608,32]{0,1:T(8,128)}, f32[4608,32]{0,1:T(8,128)S(1)}, u32[]{:S(2)}) copy-start(f32[4608,32]{0,1:T(8,128)S(1)} %get-tuple-element.81) | copy-start | bytes 1769476
  258.8 227.7 %all-gather.9.cloned.1.call-start = ((), (), s32[]{:S(2)}) async-start(), calls=%async_computation.7 | async-start | bytes 2654208 | tf_op jit(solution)/shard_map/all_gather | solution.py:114
  455.1 99.4 %reduce-scatter.7.cloned.1.call-start = ((), (), s32[]{:S(2)}) async-start(), calls=%async_computation.8 | async-start | bytes 5308416 | tf_op jit(solution)/shard_map/reduce_scatter | solution.py:122
  486.5 8.5 copy-start.26
  500.7 149.5 %all-gather.11.cloned.1.call-start = ((), (), s32[]{:S(2)}) async-start(), calls=%async_computation.9 | async-start | bytes 10616832 | tf_op jit(solution)/shard_map/all_gather | solution.py:129
  557.7 92.5 %copy-start.38 = (bf16[32,1024]{1,0:T(8,128)(2,1)S(1)}, bf16[32,1024]{1,0:T(8,128)(2,1)}, u32[]{:S(2)}) copy-start(bf16[32,1024]{1,0:T(8,128)(2,1)} %param.19) | copy-start | bytes 196612
  560.5 217.2 %reduce-scatter.9.cloned.1.call-start = ((), (), s32[]{:S(2)}) async-start(), calls=%async_computation.10 | async-start | bytes 5308416 | tf_op jit(solution)/shard_map/reduce_scatter | solution.py:163
  657.0 28.5 %copy-start.31 = (bf16[3,3,256,32]{2,3,1,0:T(8,128)(2,1)S(1)}, bf16[3,3,256,32]{2,3,1,0:T(8,128)(2,1)}, u32[]{:S(2)}) copy-start(bf16[3,3,256,32]{2,3,1,0:T(8,128)(2,1)} %param.17) | copy-start | bytes 442372
  725.3 52.5 %copy-start.21 = (f32[4608,32]{0,1:T(8,128)S(1)}, f32[4608,32]{0,1:T(8,128)}, u32[]{:S(2)}) copy-start(f32[4608,32]{0,1:T(8,128)} %copy-done.20) | copy-start | bytes 1769476
  725.3 52.5 %copy-start.43 = (f32[32]{0:T(128)S(1)}, f32[32]{0:T(128)}, u32[]{:S(2)}) copy-start(f32[32]{0:T(128)} %param.16) | copy-start | bytes 388
  725.3 81.7 %copy-start.33 = (bf16[1024,32]{0,1:T(8,128)(2,1)S(1)}, bf16[1024,32]{0,1:T(8,128)(2,1)}, u32[]{:S(2)}) copy-start(bf16[1024,32]{0,1:T(8,128)(2,1)} %param.15) | copy-start | bytes 196612
  725.3 275.9 %reduce-scatter.11.cloned.1.call-start = ((), (), s32[]{:S(2)}) async-start(), calls=%async_computation.11 | async-start | bytes 21233664 | tf_op jit(solution)/shard_map/reduce_scatter | solution.py:174
  814.9 284.9 %all-reduce.20.cloned.1.call-start = ((), (), s32[]{:S(2)}) async-start(), calls=%async_computation.12 | async-start | bytes 2949120 | tf_op jit(solution)/shard_map/psum | solution.py:182
  816.1 11.3 %copy-start.13 = (bf16[8,24,24,256]{3,2,1,0:T(8,128)(2,1)S(1)}, bf16[8,24,24,256]{3,2,1,0:T(8,128)(2,1)}, u32[]{:S(2)}) copy-start(bf16[8,24,24,256]{3,2,1,0:T(8,128)(2,1)} %copy-done.12) | copy-start | bytes 7077892
  816.1 12.6 %copy-start.11 = (bf16[8,24,24,256]{3,2,1,0:T(8,128)(2,1)S(1)}, bf16[8,24,24,256]{3,2,1,0:T(8,128)(2,1)}, u32[]{:S(2)}) copy-start(bf16[8,24,24,256]{3,2,1,0:T(8,128)(2,1)} %copy-done.10) | copy-start | bytes 7077892
  820.5 8.8 copy-start.9
  822.8 9.1 slice-start.3
  834.9 166.3 %copy-start.23 = (f32[24,24,128]{2,1,0:T(8,128)S(1)}, f32[24,24,128]{2,1,0:T(8,128)}, u32[]{:S(2)}) copy-start(f32[24,24,128]{2,1,0:T(8,128)} %param.13) | copy-start | bytes 884740
  834.9 166.4 %copy-start.45 = (f32[128]{0:T(128)S(1)}, f32[128]{0:T(128)}, u32[]{:S(2)}) copy-start(f32[128]{0:T(128)} %param.14) | copy-start | bytes 1540
  1054.2 51.3 %copy-start.1 = (bf16[512,1024]{1,0:T(8,128)(2,1)S(1)}, bf16[512,1024]{1,0:T(8,128)(2,1)}, u32[]{:S(2)}) copy-start(bf16[512,1024]{1,0:T(8,128)(2,1)} %param.20) | copy-start | bytes 3145732
  (32 other events, 100.6 us)
Sparse Core Ops, SparseCore 0:
  43.6 89.3 all-gather.4
  168.2 28.9 all-gather.6
  258.9 186.0 reduce-scatter.4
  455.3 31.1 all-gather.8
  500.8 53.6 reduce-scatter.6
  560.7 89.5 all-gather.10
  725.4 52.2 reduce-scatter.8
  815.0 186.1 reduce-scatter.10
  1041.2 58.5 all-reduce.19
where the time goes:
time: 1120 us; the launch traced here: 1110 us
  waiting for transfers between devices  735 us (66%)
  blocking collectives  177 us (16%)
  matrix products  87.4 us (8%)
  other arithmetic  55 us (5%)
  local copies, waits for them, and re-layouts  42.4 us (4%)
  between operations  15.1 us (1%)
    reduce_scatter x1, waiting for transfers between devices, local(): lax.psum_scatter(expand_terms, 'tensor', scatter_dimension=1, tiled=True)  185 us
    psum x6, blocking collectives, row_totals(): return lax.psum((leading, trailing), 'tensor')  167 us
    reduce_scatter x1, waiting for transfers between devices, local(): lax.psum_scatter(outer_terms, 'tensor', scatter_dimension=1, tiled=True)  164 us
    all_gather x1, waiting for transfers between devices, local(): grad_full = lax.all_gather(grad_branch, 'tensor', axis=1, tiled=True)  89.6 us
    all_gather x1, waiting for transfers between devices, local(): reduce_full = lax.all_gather(reduce_in, 'tensor', axis=1, tiled=True)  89.5 us
    reduce_scatter x1, waiting for transfers between devices, local(): lax.psum_scatter(pooled_terms, 'tensor', scatter_dimension=1, tiled=True)  53.8 us
    reduce_scatter x1, waiting for transfers between devices, local(): lax.psum_scatter(grad_window, 'tensor', scatter_dimension=1, tiled=True)  52.4 us
    psum x1, waiting for transfers between devices, local(): lax.psum(grad_place.astype(jnp.bfloat16), 'dp').astype(jnp.float32)  42.5 us
  transfers between devices with their start and end apart: 9, of which 9 were waited for; matrix products, arithmetic and copies ran while one was open for 3% of the time, Pallas kernels for 0%

commit v1 on v0

--- a/solution.py
+++ b/solution.py
@@ -4,6 +4,136 @@
 from jax.sharding import PartitionSpec as P
 
 epsilon = 1e-05
+bf16 = jnp.bfloat16
+f32 = jnp.float32
+
+
+def silu_grad(inputs):
+    gate_value = jax.nn.sigmoid(inputs)
+    return gate_value * (1.0 + inputs * (1.0 - gate_value))
+
+
+def gelu_grad(inputs):
+    below = 0.5 * (1.0 + lax.erf(inputs * 0.7071067811865476))
+    density = jnp.exp(-0.5 * inputs * inputs) * 0.3989422804014327
+    return below + inputs * density
+
+
+def dot(a, b, ca, cb):
+    return lax.dot_general(a, b, (((ca,), (cb,)), ((), ())), preferred_element_type=f32)
+
+
+def shifted(grid_values, a, b, side):
+    padded = jnp.pad(grid_values, ((1, 1), (1, 1), (0, 0)))
+    return padded[a : a + side, b : b + side].reshape(side * side, -1)
+
+
+def gather(x, axis):
+    return lax.all_gather(x, "tensor", axis=axis, tiled=True)
+
+
+def local_by_image(features, slot_live, position, gain_outer, reduce_weight, gain_middle, conv_weight, gain_inner, expand_weight, readout_weight, cotangent):
+    side = position.shape[0]
+    half = side // 2
+    cells = half * half
+    spots = side * side
+    share = features.shape[0]
+    rows = features.shape[1]
+    images = rows // spots
+    parts = lax.axis_size("tensor")
+    me = lax.axis_index("tensor")
+    channels = share * parts
+    hs = reduce_weight.shape[1]
+    hidden_width = hs * parts
+    live = slot_live.astype(f32)
+
+    w_mine = lax.all_to_all(reduce_weight, "tensor", split_axis=0, concat_axis=1, tiled=True)
+    conv_full = gather(conv_weight, 3).reshape(9, hidden_width, hidden_width)
+    expand_full = gather(expand_weight, 0)
+    gm = gather(gain_middle, 0)
+    gi = gather(gain_inner, 0)
+    go = gain_outer[:, None]
+
+    placed = (features.astype(f32).reshape(share, images, spots) + position.reshape(spots, share).T[:, None, :]).reshape(share, rows)
+    m_mine = jnp.mean(placed, axis=0)
+    centred = placed - m_mine
+    q_mine = jnp.sum(centred * centred, axis=0)
+    part = dot((centred * go).astype(bf16), w_mine, 0, 0)
+    reduced0 = lax.psum_scatter(part.astype(bf16), "tensor", scatter_dimension=0, tiled=True).astype(f32)
+    stats = lax.all_to_all(jnp.stack([m_mine, q_mine]), "tensor", split_axis=1, concat_axis=0, tiled=True).reshape(parts, 2, spots)
+    m_t, q_t = stats[:, 0], stats[:, 1]
+    colsum = gather(jnp.sum(w_mine.astype(f32) * go, axis=0)[None], 0)
+    mean = jnp.mean(m_t, axis=0)
+    dm = m_t - mean
+    var = (jnp.sum(q_t, axis=0) + share * jnp.sum(dm * dm, axis=0)) / channels
+    rstd = lax.rsqrt(var + epsilon)
+    corr = lax.dot_general(dm, colsum, (((0,), (0,)), ((), ())), precision=lax.Precision.HIGHEST, preferred_element_type=f32)
+    reduced = rstd[:, None] * (reduced0 + corr)
+
+    def norm(v, g):
+        c = jnp.mean(v, axis=1, keepdims=True)
+        s = v - c
+        r = lax.rsqrt(jnp.mean(s * s, axis=1, keepdims=True) + epsilon)
+        return s * r, r, s * r * g
+
+    xm, rm, zm = norm(reduced, gm)
+    hidden = jax.nn.silu(zm).astype(bf16)
+    hidden_grid = hidden.reshape(side, side, hidden_width)
+    convolved = sum(dot(shifted(hidden_grid, t // 3, t % 3, side), conv_full[t], 1, 0) for t in range(9))
+    xi, ri, zi = norm(convolved, gi)
+    activated = jax.nn.silu(zi).astype(bf16)
+    act_cells = jnp.mean(activated.astype(f32).reshape(half, 2, half, 2, hidden_width), axis=(1, 3)).reshape(cells, hidden_width)
+    act_all = gather(act_cells.astype(bf16), 0)
+    act_live = (act_all.astype(f32) * jnp.repeat(live, cells)[:, None]).astype(bf16)
+
+    placed_cells = jnp.mean(placed.reshape(share, images, half, 2, half, 2), axis=(3, 5)).reshape(share, images * cells).T
+    placed_pool = gather(placed_cells.astype(bf16), 1)
+    pooled = (placed_pool.astype(f32) + dot(act_live, expand_full, 1, 0)).astype(bf16)
+    before = dot(pooled, readout_weight, 1, 1)
+    readout = jax.nn.gelu(before, approximate=False).astype(bf16).T
+    grad_before = (cotangent.T.astype(f32) * gelu_grad(before)).astype(bf16)
+    grad_readout = dot(grad_before, pooled, 0, 0)
+    terms = dot(grad_before, readout_weight, 1, 0)
+    act_terms = dot(terms.astype(bf16), expand_full, 1, 1)
+    grad_act = lax.psum_scatter(act_terms.astype(bf16), "tensor", scatter_dimension=0, tiled=True).astype(f32)
+    grad_act = grad_act * (0.25 * live[me])
+    grad_pooled = lax.psum_scatter(terms.astype(bf16), "tensor", scatter_dimension=1, tiled=True)
+    grad_expand = 1.0 * dot(act_live, grad_pooled, 0, 0)
+    grad_expand = lax.all_to_all(grad_expand.astype(bf16), "tensor", split_axis=0, concat_axis=1, tiled=True)
+
+    def norm_back(dy, xhat, r, g):
+        dx = dy * g
+        return r * (dx - jnp.mean(dx, axis=1, keepdims=True) - xhat * jnp.mean(dx * xhat, axis=1, keepdims=True)), jnp.sum(dy * xhat, axis=0)
+
+    ga_rows = jnp.broadcast_to(grad_act.reshape(half, 1, half, 1, hidden_width), (half, 2, half, 2, hidden_width)).reshape(spots, hidden_width)
+    gc, g_gi = norm_back(ga_rows * silu_grad(zi), xi, ri, gi)
+    gc = gc.astype(bf16)
+    gc_grid = gc.reshape(side, side, hidden_width)
+    grad_conv = jnp.stack([dot(shifted(hidden_grid, t // 3, t % 3, side), gc, 0, 0) for t in range(9)])
+    grad_hidden = sum(dot(shifted(gc_grid, 2 - t // 3, 2 - t % 3, side), conv_full[t], 1, 1) for t in range(9))
+    gr, g_gm = norm_back(grad_hidden * silu_grad(zm), xm, rm, gm)
+    gr = gr.astype(bf16)
+
+    wg = jnp.sum(colsum, axis=0)
+    s1 = dot(gr.astype(f32), wg[:, None], 1, 0)[:, 0] / channels
+    s2 = jnp.sum(gr.astype(f32) * reduced, axis=1) / channels
+    gr_all = gather(gr, 0)
+    row_stats = gather(jnp.stack([mean, rstd, s1, s2]), 1)
+    xhat = (placed - row_stats[0]) * row_stats[1]
+    gn = dot(w_mine, gr_all, 1, 1)
+    grad_in = row_stats[1] * (gn * go - row_stats[2] - xhat * row_stats[3])
+    g_go = jnp.sum(gn * xhat, axis=1)
+    grad_reduce = dot((xhat * go).astype(bf16), gr_all, 1, 0)
+    grad_reduce = lax.all_to_all(grad_reduce.astype(bf16), "tensor", split_axis=1, concat_axis=0, tiled=True)
+    spread = (0.25 * grad_pooled.astype(f32)).T.reshape(share, images, half, 1, half, 1)
+    grad_features = jnp.broadcast_to(spread, (share, images, half, 2, half, 2)).reshape(share, rows) + grad_in
+    grad_position = jnp.sum(grad_features.reshape(share, images, spots), axis=1).T.reshape(side, side, share)
+    g_conv = lax.psum_scatter(grad_conv.astype(bf16), "tensor", scatter_dimension=2, tiled=True).reshape(conv_weight.shape)
+    g_gm = lax.psum_scatter(g_gm.astype(f32), "tensor", scatter_dimension=0, tiled=True)
+    g_gi = lax.psum_scatter(g_gi.astype(f32), "tensor", scatter_dimension=0, tiled=True)
+    out = [grad_position, g_go, grad_reduce, g_gm, g_conv, g_gi, grad_expand, grad_readout]
+    out = [lax.psum(o.astype(bf16), "dp").astype(f32) for o in out]
+    return (readout, grad_features, *out)
 
 
 def row_totals(leading, trailing):
@@ -31,12 +161,12 @@
     return (grad_in, gain_grad)
 
 
-def silu_grad(inputs):
+def silu_slope(inputs):
     gate_value = jax.nn.sigmoid(inputs)
     return gate_value * (1.0 + inputs * (1.0 - gate_value))
 
 
-def gelu_grad(inputs):
+def gelu_slope(inputs):
     below = 0.5 * (1.0 + lax.erf(inputs * 0.7071067811865476))
     density = jnp.exp(-0.5 * inputs * inputs) * 0.3989422804014327
     return below + inputs * density
@@ -56,7 +186,7 @@
     ].reshape(images * grid_side * grid_side, breadth)
 
 
-def local(
+def local_by_hidden(
     features,
     slot_live,
     position,
@@ -116,7 +246,7 @@
         pooled_full, readout_weight, (((1,), (1,)), ((), ())), preferred_element_type=jnp.float32
     )
     readout = jax.nn.gelu(before, approximate=False).astype(jnp.bfloat16).T
-    grad_before = (cotangent.T.astype(jnp.float32) * gelu_grad(before)).astype(jnp.bfloat16)
+    grad_before = (cotangent.T.astype(jnp.float32) * gelu_slope(before)).astype(jnp.bfloat16)
     grad_readout = contract_rows(grad_before, pooled_full)
     pooled_terms = jnp.dot(grad_before, readout_weight, preferred_element_type=jnp.float32)
     grad_pooled = lax.psum_scatter(pooled_terms, "tensor", scatter_dimension=1, tiled=True)
@@ -130,7 +260,7 @@
     grad_expand = contract_rows(activated, grad_full)
     grad_activated = jnp.dot(grad_full, expand_weight.T, preferred_element_type=jnp.float32)
     grad_convolved, grad_gain_inner = norm_backward(
-        grad_activated * silu_grad(shaped_inner),
+        grad_activated * silu_slope(shaped_inner),
         normed_inner,
         scaled_inner,
         gain_inner,
@@ -162,7 +292,7 @@
     )
     grad_hidden = lax.psum_scatter(grad_window, "tensor", scatter_dimension=1, tiled=True)
     grad_reduced, grad_gain_middle = norm_backward(
-        grad_hidden * silu_grad(shaped_middle),
+        grad_hidden * silu_slope(shaped_middle),
         normed_middle,
         scaled_middle,
         gain_middle,
@@ -203,33 +333,14 @@
 
 
 def solution(mesh):
-    return jax.shard_map(
-        local,
-        mesh=mesh,
-        in_specs=(
-            P("tensor", "dp"),
-            P("dp"),
-            P(None, None, "tensor"),
-            P("tensor"),
-            P(None, "tensor"),
-            P("tensor"),
-            P(None, None, None, "tensor"),
-            P("tensor"),
-            P("tensor", None),
-            P("tensor", None),
-            P("tensor", "dp"),
-        ),
-        out_specs=(
-            P("tensor", "dp"),
-            P("tensor", "dp"),
-            P(None, None, "tensor"),
-            P("tensor"),
-            P(None, "tensor"),
-            P("tensor"),
-            P(None, None, None, "tensor"),
-            P("tensor"),
-            P("tensor", None),
-            P("tensor", None),
-        ),
-        check_vma=False,
-    )
+    parts, groups = mesh.shape["tensor"], mesh.shape["dp"]
+    specs = (P("tensor", "dp"), P("dp"), P(None, None, "tensor"), P("tensor"), P(None, "tensor"), P("tensor"), P(None, None, None, "tensor"), P("tensor"), P("tensor", None), P("tensor", None), P("tensor", "dp"))
+
+    def whole(*arrays):
+        by_image = arrays[1].shape[0] == parts * groups
+        return jax.shard_map(
+            local_by_image if by_image else local_by_hidden, mesh=mesh, in_specs=specs,
+            out_specs=(P("tensor", "dp"), P("tensor", "dp"), *specs[2:10]), check_vma=False,
+        )(*arrays)
+
+    return whole

time: 1120 us -> 391 us (0.35)
  waiting for transfers between devices: 735 us -> 142 us
  blocking collectives: 177 us -> 101 us
  matrix products: 87.4 us -> 46.9 us
  other arithmetic: 55 us -> 27.9 us
  starting transfers between devices: 1.07 us -> 17.2 us
    reduce_scatter x4 -> x3, waiting for transfers between devices: 456 us -> 33.7 us  [the longest x1 28.3 us: local_by_image(): lax.psum_scatter(act_terms.astype(bf16), 'tensor', scatter_dimension=0, t...]
    all_gather x4 -> x3, waiting for transfers between devices: 236 us -> 35.5 us  [gather(): return lax.all_gather(x, 'tensor', axis=axis, tiled=True)]
    psum x7 -> x1, blocking collectives: 177 us -> 10.1 us  [local_by_image(): out = [lax.psum(o.astype(bf16), 'dp').astype(f32) for o in out]]
    all_gather x0 -> x4, blocking collectives: none -> 60.2 us  [gather(): return lax.all_gather(x, 'tensor', axis=axis, tiled=True)]
    dot_general x36 -> x38, matrix products: 87.4 us -> 46.9 us  [the longest x37 45.2 us: dot(): lax.dot_general(a, b, (((ca,), (cb,)), ((), ())), preferred_element_type=...]
    unnamed x9, waiting for transfers between devices: 0.15 us -> 36.5 us
    unnamed x0 -> x2, blocking collectives: none -> 30.7 us
    add x4 -> x0, other arithmetic: 23.9 us -> none  [the longest x2 13.8 us: local(): grad_padded + jnp.pad(tap_back.reshape(images, grid_side, grid_side, hidd...]
  transfers between devices with their start and end apart: 9 -> 12, of which waited for: 9 -> 9; matrix products, arithmetic and copies ran while one was open for 3% -> 16% of each run, Pallas kernels for 0% -> 0%
where the time goes in v1:
time: 391 us; the launch traced here: 389 us
  waiting for transfers between devices  142 us (36%)
  blocking collectives  101 us (26%)
  matrix products  46.9 us (12%)
  local copies, waits for them, and re-layouts  37.2 us (10%)
  other arithmetic  27.9 us (7%)
  starting transfers between devices  17.2 us (4%)
  between operations  17.1 us (4%)
    all_gather x4, blocking collectives, gather(): return lax.all_gather(x, 'tensor', axis=axis, tiled=True)  60.2 us
    dot_general x37, matrix products, dot(): lax.dot_general(a, b, (((ca,), (cb,)), ((), ())), preferred_element_type=...  45.2 us
    unnamed x9, waiting for transfers between devices  36.5 us
    all_gather x3, waiting for transfers between devices, gather(): return lax.all_gather(x, 'tensor', axis=axis, tiled=True)  35.5 us
    unnamed x2, blocking collectives  30.7 us
    psum x1, waiting for transfers between devices, local_by_image(): out = [lax.psum(o.astype(bf16), 'dp').astype(f32) for o in out]  30.3 us
    reduce_scatter x1, waiting for transfers between devices, local_by_image(): lax.psum_scatter(act_terms.astype(bf16), 'tensor', scatter_dimension=0, t...  28.3 us
    unnamed x125, local copies, waits for them, and re-layouts  18.2 us
  transfers between devices with their start and end apart: 12, of which 9 were waited for; matrix products, arithmetic and copies ran while one was open for 16% of the time, Pallas kernels for 0%

profile of v1, /device:TPU:0, one launch (start us, length us, event | category | flops | bytes accessed | tf_op | source)
XLA Modules:
  0.0 389.3 jit_solution(2976403232299202088)
XLA Ops:
  8.8 6.3 %all-to-all-start.1 = ((bf16[8,128,32]{1,2,0:T(8,128)(2,1)}), bf16[8,128,32]{1,2,0:T(8,128)(2,1)S(1)}, u32[]{:S(2)}, u32[]{:S(2)}) async-start(bf16[8,128,32]{1,2,0:T(8,128)(2,1)} %copy_bitcast_fusion.2), calls=%async_computation.1 | async-start | bytes 131072 | tf_op jit(solution)/shard_map/all_to_all | solution.py:50
  21.0 3.4 convolution_convert_fusion
  26.1 3.3 all-to-all-start
  29.5 2.2 add_reduce_fusion
  32.7 18.7 %all_gather.33 = bf16[256,1024]{1,0:T(8,128)(2,1)} all-gather(bf16[32,1024]{1,0:T(8,128)(2,1)S(1)} %copy-done.37), channel_id=1, replica_groups=mesh['dp'=4,'tensor'=8] {'tensor'}, dimensions={0}, use_global_device_ids=true | all-gather | bytes 589824 | tf_op jit(solution)/shard_map/all_gather | solution.py:32
  52.2 2.4 copy.60
  56.3 16.9 %all-reduce.7 = (f32[256]{0:T(256)S(1)}, f32[256]{0:T(256)S(1)}) all-reduce(f32[256]{0:T(256)S(1)} %dynamic-update-slice, f32[256]{0:T(256)S(1)} %dynamic-update-slice.1), channel_id=1, replica_groups=mesh['dp'=4,'tensor'=8] {'tensor'}, use_global_device_ids=true, to_apply=%add.2 | all-reduce | flops 512 | bytes 4096
  73.6 8.6 %all-gather = f32[8,1,256]{2,1,0:T(1,128)S(1)} all-gather(f32[1,1,256]{2,1,0:T(1,128)S(1)} %reshape.319), channel_id=1, replica_groups=mesh['dp'=4,'tensor'=8] {'tensor'}, dimensions={0}, use_global_device_ids=true | all-gather | bytes 9216 | tf_op jit(solution)/shard_map/all_gather | solution.py:32
  86.0 2.4 all-gather.8.cloned.1.call-done
  94.9 2.2 reshape.311
  97.1 2.2 reduce_sum.209
  101.8 18.9 %all_gather.32 = bf16[1152,256]{1,0:T(8,128)(2,1)} all-gather(bf16[144,256]{1,0:T(8,128)(2,1)S(1)} %convert_element_type.184), channel_id=1, replica_groups=mesh['dp'=4,'tensor'=8] {'tensor'}, dimensions={0}, use_global_device_ids=true | all-gather | bytes 663552 | tf_op jit(solution)/shard_map/all_gather | solution.py:32
  120.6 7.1 %all-gather.6.cloned.1.call-done = bf16[1152,1024]{1,0:T(8,128)(2,1)} async-done(((bf16[1152,128]{1,0:T(8,128)(2,1)}), bf16[1152,1024]{1,0:T(8,128)(2,1)}) %all-gather.6.cloned.1.call-update) | async-done | bytes 2359312 | tf_op jit(solution)/shard_map/all_gather | solution.py:32
  127.8 2.9 fusion
  130.7 7.4 %fusion.3 = (bf16[512,1152]{0,1:T(8,128)(2,1)}, f32[1152,512]{1,0:T(8,128)S(1)}) fusion(bf16[1152,1024]{1,0:T(8,128)(2,1)S(1)} %fusion, bf16[512,1024]{1,0:T(8,128)(2,1)S(1)} %copy-done), kind=kOutput, calls=%fused_computation.10 | convolution fusion | flops 1246298112 | bytes 6946816 | tf_op jit(solution)/shard_map/dot_general | solution.py:23
  145.2 28.3 %reduce-scatter.9.cloned.1.call-done = bf16[144,256]{1,0:T(8,128)(2,1)} async-done(((bf16[1152,256]{1,0:T(8,128)(2,1)}), bf16[144,256]{1,0:T(8,128)(2,1)}) %reduce-scatter.9.cloned.1.call-update) | async-done | bytes 73744 | tf_op jit(solution)/shard_map/reduce_scatter | solution.py:98
  186.7 4.3 %copy.64 = bf16[9,256,256]{1,0,2:T(8,128)(2,1)} copy(bf16[9,256,256]{2,1,0:T(8,128)(2,1)} %fusion.45) | data formatting | bytes 2359296 | tf_op jit(solution)/shard_map/stack | solution.py:112
  191.1 4.3 %copy.69 = bf16[1152,1024]{0,1:T(8,128)(2,1)} copy(bf16[1152,1024]{1,0:T(8,128)(2,1)} %copy-done.14) | data formatting | bytes 4718592
  200.6 4.6 %convolution_convert_fusion.3 = bf16[512,1024]{1,0:T(8,128)(2,1)} fusion(bf16[1152,512]{1,0:T(8,128)(2,1)} %copy-done.7, bf16[1152,1024]{1,0:T(8,128)(2,1)} %copy-done.4), kind=kOutput, calls=%fused_computation.46 | convolution fusion | flops 1208483840 | bytes 4587520 | tf_op jit(solution)/shard_map/dot_general | solution.py:23
  205.5 14.0 %all-gather.1 = f32[8,576,4]{1,2,0:T(4,128)S(1)} all-gather(f32[1,576,4]{1,2,0:T(4,128)S(1)} %maximum_bitcast_fusion), channel_id=1, replica_groups=mesh['dp'=4,'tensor'=8] {'tensor'}, dimensions={0}, use_global_device_ids=true | all-gather | bytes 82944 | tf_op jit(solution)/shard_map/all_gather | solution.py:32
  219.8 5.4 %reduce-scatter.11.cloned.1.call-done = bf16[9,256,32]{1,0,2:T(8,128)(2,1)} async-done(((bf16[9,256,256]{1,0,2:T(8,128)(2,1)}), bf16[9,256,32]{1,0,2:T(8,128)(2,1)}) %reduce-scatter.11.cloned.1.call-update) | async-done | bytes 147472 | tf_op jit(solution)/shard_map/reduce_scatter | solution.py:131
  226.9 35.7 %reduce-scatter.13.cloned.1.call-done = bf16[128,1152]{1,0:T(8,128)(2,1)} async-done(((bf16[1024,1152]{1,0:T(8,128)(2,1)}), bf16[128,1152]{1,0:T(8,128)(2,1)}) %reduce-scatter.13.cloned.1.call-update) | async-done | bytes 294928
  266.0 3.6 all-to-all-start.3
  269.7 26.0 %all-gather.10.cloned.1.call-done = bf16[4608,256]{1,0:T(8,128)(2,1)} async-done(((bf16[576,256]{1,0:T(8,128)(2,1)}), bf16[4608,256]{1,0:T(8,128)(2,1)}) %all-gather.10.cloned.1.call-update) | async-done | bytes 2359312 | tf_op jit(solution)/shard_map/all_gather | solution.py:32
  297.4 4.0 %multiply_reduce_fusion = (bf16[128]{0:T(256)(128)(2,1)S(1)}, f32[128,4608]{0,1:T(8,128)}, bf16[128,4608]{0,1:T(8,128)(2,1)S(1)}) fusion(bf16[128,4608]{0,1:T(8,128)(2,1)S(1)} %copy.56, f32[4608]{0:T(1024)S(1)} %get-tuple-element.68, f32[4608]{0:T(1024)S(1)} %get-tuple-element.66, f32[128,576]{0,1:T(8,128)S(1)} %bitcast.309, f32[128,4608]{0,1:T(8,128)S(1)} %bitcast.304, ...), kind=kOutput, calls=%fused_computation.24 | convolution fusion | flops 310247296 | bytes 9872128 | tf_op jit(solution)/shard_map/dot_general | solution.py:23
  302.7 3.4 all-to-all-start.2
  307.6 4.4 %all-to-all-done.2 = bf16[128,8,32]{0,2,1:T(8,128)(2,1)S(1)} async-done(((bf16[128,8,32]{0,2,1:T(8,128)(2,1)}), bf16[128,8,32]{0,2,1:T(8,128)(2,1)S(1)}, u32[]{:S(2)}, u32[]{:S(2)}) %all-to-all-start.2) | async-done | bytes 65568 | tf_op jit(solution)/shard_map/all_to_all | solution.py:127
  313.2 2.4 copy.67
  315.6 13.8 %all-reduce.6 = (bf16[256]{0:T(256)(128)(2,1)S(1)}, bf16[256]{0:T(256)(128)(2,1)S(1)}) all-reduce(f32[256]{0:T(256)S(1)} %get-tuple-element.62, f32[256]{0:T(256)S(1)} %get-tuple-element.60), channel_id=5, replica_groups=mesh['dp'=4,'tensor'=8] {'tensor'}, use_global_device_ids=true, to_apply=%region_27.28.clone | all-reduce | flops 512 | bytes 3072
  331.5 10.1 %all-reduce.8 = (bf16[128]{0:T(256)(128)(2,1)S(1)}, bf16[32]{0:T(256)(128)(2,1)S(1)}, bf16[32]{0:T(256)(128)(2,1)S(1)}) all-reduce(bf16[128]{0:T(256)(128)(2,1)S(1)} %get-tuple-element.87, bf16[32]{0:T(256)(128)(2,1)S(1)} %dynamic-slice.9, bf16[32]{0:T(256)(128)(2,1)S(1)} %dynamic-slice.8), channel_id=1, replica_groups=mesh['dp'=4,'tensor'=8] {'dp'}, use_global_device_ids=true, to_apply=%region_24.25 | all-reduce | flops 192 | bytes 768 | tf_op jit(solution)/shard_map/psum | solution.py:135
  343.1 30.3 %all-reduce.12.cloned.1.call-done = (bf16[24,24,128]{2,1,0:T(8,128)(2,1)}, bf16[1024,32]{0,1:T(8,128)(2,1)}, bf16[3,3,256,32]{2,3,1,0:T(8,128)(2,1)}, bf16[32,1024]{1,0:T(8,128)(2,1)}, bf16[512,1024]{1,0:T(8,128)(2,1)}) async-done(((bf16[24,24,128]{2,1,0:T(8,128)(2,1)}, bf16[1024,32]{0,1:T(8,128)(2,1)}, bf16[3,3,256,32]{2,3,1,0:T(8,128)(2,1)}, bf16[32,1024]{1,0:T(8,128)(2,1)}, bf16[512,1024]{1,0:T(8,128)(2,1)}), ...) | async-done | bytes 1474576 | tf_op jit(solution)/shard_map/psum | solution.py:135
  379.7 2.8 convert_element_type.217
  (241 shorter events, 70.0 us)
Async XLA Ops:
  7.2 123.5 %copy-start = (bf16[512,1024]{1,0:T(8,128)(2,1)S(1)}, bf16[512,1024]{1,0:T(8,128)(2,1)}, u32[]{:S(2)}) copy-start(bf16[512,1024]{1,0:T(8,128)(2,1)} %param.20) | copy-start | bytes 3145732
  7.2 9.7 %copy-start.5 = (f32[24,24,128]{2,1,0:T(8,128)S(1)}, f32[24,24,128]{2,1,0:T(8,128)}, u32[]{:S(2)}) copy-start(f32[24,24,128]{2,1,0:T(8,128)} %param.13) | copy-start | bytes 884740
  7.2 10.4 %copy-start.45 = (f32[128]{0:T(128)S(1)}, f32[128]{0:T(128)}, u32[]{:S(2)}) copy-start(f32[128]{0:T(128)} %param.14) | copy-start | bytes 1540
  8.8 12.2 %all-to-all-start.1 = ((bf16[8,128,32]{1,2,0:T(8,128)(2,1)}), bf16[8,128,32]{1,2,0:T(8,128)(2,1)S(1)}, u32[]{:S(2)}, u32[]{:S(2)}) async-start(bf16[8,128,32]{1,2,0:T(8,128)(2,1)} %copy_bitcast_fusion.2), calls=%async_computation.1 | async-start | bytes 131072 | tf_op jit(solution)/shard_map/all_to_all | solution.py:50
  15.1 67.1 %reduce-scatter.7.cloned.1.call-start = ((), (), s32[]{:S(2)}) async-start(), calls=%async_computation.9 | async-start | bytes 2654208 | tf_op jit(solution)/shard_map/reduce_scatter | solution.py:62
  24.5 63.9 %all-gather.8.cloned.1.call-start = ((), (), s32[]{:S(2)}) async-start(), calls=%async_computation.10 | async-start | bytes 1327104 | tf_op jit(solution)/shard_map/all_gather | solution.py:32
  25.3 7.5 %copy-start.37 = (bf16[32,1024]{1,0:T(8,128)(2,1)S(1)}, bf16[32,1024]{1,0:T(8,128)(2,1)}, u32[]{:S(2)}) copy-start(bf16[32,1024]{1,0:T(8,128)(2,1)} %param.19) | copy-start | bytes 196612
  26.1 47.1 %all-to-all-start = ((f32[2,8,576]{2,0,1:T(2,128)}), f32[2,8,576]{2,0,1:T(2,128)S(1)}, u32[]{:S(2)}, u32[]{:S(2)}) async-start(f32[2,8,576]{2,0,1:T(2,128)} %pad_maximum_fusion), calls=%async_computation | async-start | bytes 81920 | tf_op jit(solution)/shard_map/all_to_all | solution.py:63
  29.5 98.3 %all-gather.6.cloned.1.call-start = ((), (), s32[]{:S(2)}) async-start(), calls=%async_computation.8 | async-start | bytes 2654208 | tf_op jit(solution)/shard_map/all_gather | solution.py:32
  29.5 22.0 %copy-start.52 = (s32[8]{0:T(128)S(1)}, s32[8]{0:T(128)}, u32[]{:S(2)}) copy-start(s32[8]{0:T(128)} %param.12) | copy-start | bytes 100
  31.8 22.9 %copy-start.49 = (u32[32]{0:T(128)S(1)}, u32[32]{0:T(128)}, u32[]{:S(2)}) copy-start(u32[32]{0:T(128)} %constant.120) | copy-start | bytes 388
  31.8 24.1 %copy-start.53 = (f32[32]{0:T(128)S(1)}, f32[32]{0:T(128)}, u32[]{:S(2)}) copy-start(f32[32]{0:T(128)} %param.16) | copy-start | bytes 388
  31.8 24.3 %copy-start.54 = (f32[32]{0:T(128)S(1)}, f32[32]{0:T(128)}, u32[]{:S(2)}) copy-start(f32[32]{0:T(128)} %param.18) | copy-start | bytes 388
  32.7 140.8 %reduce-scatter.9.cloned.1.call-start = ((), (), s32[]{:S(2)}) async-start(), calls=%async_computation.11 | async-start | bytes 663552 | tf_op jit(solution)/shard_map/reduce_scatter | solution.py:98
  51.5 30.7 %copy-start.50 = (f32[8]{0:T(128)}, f32[8]{0:T(128)S(1)}, u32[]{:S(2)}) copy-start(f32[8]{0:T(128)S(1)} %convert_element_type.186) | copy-start | bytes 100
  73.2 12.8 %copy-start.47 = (f32[256]{0:T(256)}, f32[256]{0:T(256)S(1)}, u32[]{:S(2)}) copy-start(f32[256]{0:T(256)S(1)} %get-tuple-element.74) | copy-start | bytes 3076
  73.2 20.5 %copy-start.43 = (f32[256]{0:T(256)}, f32[256]{0:T(256)S(1)}, u32[]{:S(2)}) copy-start(f32[256]{0:T(256)S(1)} %get-tuple-element.75) | copy-start | bytes 3076
  73.3 10.9 %copy-start.35 = (f32[576]{0:T(1024)}, f32[576]{0:T(1024)S(1)}, u32[]{:S(2)}) copy-start(f32[576]{0:T(1024)S(1)} %broadcast_multiply_fusion.9) | copy-start | bytes 6916
  73.4 10.9 %copy-start.40 = (f32[576]{0:T(1024)}, f32[576]{0:T(1024)S(1)}, u32[]{:S(2)}) copy-start(f32[576]{0:T(1024)S(1)} %add_rsqrt_fusion.2) | copy-start | bytes 6916
  143.6 32.2 %copy-start.34 = (f32[576]{0:T(1024)S(1)}, f32[576]{0:T(1024)}, u32[]{:S(2)}) copy-start(f32[576]{0:T(1024)} %copy-done.33) | copy-start | bytes 6916
  143.6 32.2 %copy-start.44 = (f32[256]{0:T(256)S(1)}, f32[256]{0:T(256)}, u32[]{:S(2)}) copy-start(f32[256]{0:T(256)} %copy-done.43) | copy-start | bytes 3076
  143.6 81.6 %reduce-scatter.11.cloned.1.call-start = ((), (), s32[]{:S(2)}) async-start(), calls=%async_computation.13 | async-start | bytes 2359296 | tf_op jit(solution)/shard_map/reduce_scatter | solution.py:131
  191.0 71.6 %reduce-scatter.13.cloned.1.call-start = ((), (), s32[]{:S(2)}) async-start(), calls=%async_computation.14 | async-start | bytes 2654208
  195.5 100.2 %all-gather.10.cloned.1.call-start = ((), (), s32[]{:S(2)}) async-start(), calls=%async_computation.12 | async-start | bytes 2654208 | tf_op jit(solution)/shard_map/all_gather | solution.py:32
  200.6 63.1 %copy-start.15 = (bf16[1152,256]{1,0:T(8,128)(2,1)S(1)}, bf16[1152,256]{1,0:T(8,128)(2,1)}, u32[]{:S(2)}) copy-start(bf16[1152,256]{1,0:T(8,128)(2,1)} %all_gather.32) | copy-start | bytes 1769476
  200.6 63.1 %copy-start.42 = (f32[1152]{0:T(1024)S(1)}, f32[1152]{0:T(1024)}, u32[]{:S(2)}) copy-start(f32[1152]{0:T(1024)} %mul.311) | copy-start | bytes 13828
  266.0 36.7 %all-to-all-start.3 = ((bf16[8,32,128]{2,1,0:T(8,128)(2,1)}), bf16[8,32,128]{2,1,0:T(8,128)(2,1)S(1)}, u32[]{:S(2)}, u32[]{:S(2)}) async-start(bf16[8,32,128]{2,1,0:T(8,128)(2,1)} %bitcast.66), calls=%async_computation.6 | async-start | bytes 131072 | tf_op jit(solution)/shard_map/all_to_all | solution.py:102
  269.6 26.7 %copy-start.6 = (f32[24,24,128]{2,1,0:T(8,128)S(1)}, f32[24,24,128]{2,1,0:T(8,128)}, u32[]{:S(2)}) copy-start(f32[24,24,128]{2,1,0:T(8,128)} %param.13) | copy-start | bytes 884740
  269.6 26.7 %copy-start.46 = (f32[128]{0:T(128)S(1)}, f32[128]{0:T(128)}, u32[]{:S(2)}) copy-start(f32[128]{0:T(128)} %param.14) | copy-start | bytes 1540
  302.7 9.2 %all-to-all-start.2 = ((bf16[128,8,32]{0,2,1:T(8,128)(2,1)}), bf16[128,8,32]{0,2,1:T(8,128)(2,1)S(1)}, u32[]{:S(2)}, u32[]{:S(2)}) async-start(bf16[128,8,32]{0,2,1:T(8,128)(2,1)} %bitcast.54), calls=%async_computation.4 | async-start | bytes 131072 | tf_op jit(solution)/shard_map/all_to_all | solution.py:127
  306.1 67.3 %all-reduce.12.cloned.1.call-start = ((), (), s32[]{:S(2)}) async-start(), calls=%async_computation.15 | async-start | bytes 2949120 | tf_op jit(solution)/shard_map/psum | solution.py:135
  329.5 53.0 %copy-start.1 = (bf16[512,1024]{1,0:T(8,128)(2,1)S(1)}, bf16[512,1024]{1,0:T(8,128)(2,1)}, u32[]{:S(2)}) copy-start(bf16[512,1024]{1,0:T(8,128)(2,1)} %param.20) | copy-start | bytes 3145732
  (35 other events, 121.6 us)
Sparse Core Ops, SparseCore 0:
  24.6 39.7 reduce-scatter.6
  66.0 22.3 all-gather.7
  90.6 37.1 all-gather.5
  143.8 29.6 reduce-scatter.8
  191.2 33.9 reduce-scatter.10
  227.4 35.1 reduce-scatter.12
  264.8 30.8 all-gather.9
  312.7 60.6 all-reduce.11

commit v2 on v0

--- a/solution.py
+++ b/solution.py
@@ -1,9 +1,493 @@
 import jax
 import jax.numpy as jnp
 from jax import lax
+from jax.experimental import pallas as pl
+from jax.experimental.pallas import tpu as pltpu
 from jax.sharding import PartitionSpec as P
 
 epsilon = 1e-05
+bf16 = jnp.bfloat16
+f32 = jnp.float32
+COPIES = 112
+
+MESH = pl.DeviceIdType.MESH
+HIGHEST = lax.Precision.HIGHEST
+
+
+def mm(a, b, ca, cb, precision=None):
+    return lax.dot_general(a, b, (((ca,), (cb,)), ((), ())), precision=precision, preferred_element_type=f32)
+
+
+def split(x):
+    high = x.astype(bf16)
+    return high, (x - high.astype(f32)).astype(bf16)
+
+
+def eye(n, dtype=bf16):
+    return (lax.broadcasted_iota(jnp.int32, (n, n), 0) == lax.broadcasted_iota(jnp.int32, (n, n), 1)).astype(f32).astype(dtype)
+
+
+def pool_wide():
+    spot = lax.broadcasted_iota(jnp.int32, (144, 768), 1)
+    cell = lax.broadcasted_iota(jnp.int32, (144, 768), 0)
+    i, j = spot >> 5, spot & 31
+    return jnp.where(((i >> 1) * 12 + (j >> 1) == cell) & (j < 24), 0.25, 0.0).astype(bf16)
+
+
+def pool_pair():
+    spot = lax.broadcasted_iota(jnp.int32, (288, 1152), 1)
+    cell = lax.broadcasted_iota(jnp.int32, (288, 1152), 0)
+    i = (spot * 2731) >> 16
+    j = spot - i * 24
+    return jnp.where((i >> 1) * 12 + (j >> 1) == cell, 0.25, 0.0).astype(bf16)
+
+
+def norm_rows(v):
+    s = v - jnp.mean(v, axis=1, keepdims=True)
+    r = lax.rsqrt(jnp.mean(s * s, axis=1, keepdims=True) + epsilon)
+    return s * r, r
+
+
+def norm_rows_back(dx, xhat, r):
+    return r * (dx - jnp.mean(dx, axis=1, keepdims=True) - xhat * jnp.mean(dx * xhat, axis=1, keepdims=True))
+
+
+def kernel(
+    features, slot_live, position, gain_outer, reduce_weight, gain_middle, conv_weight, gain_inner, expand_weight, readout_weight, cotangent,
+    readout_o, gfeat_o, gpos_o, gexp_o, gred_o, gconv_o, gread_o,
+    WBLK, WT, WC, CB, WQ, WB, WF, MT, POOL, PLC, XW, XK, ST, SR, QF, QS, QO, QR, RED, HB, GB,
+    XM, ZM, RM, XI, ZI, RI, ACT, ACL, PP, POOLED, BEF, GBT, TE, TR, ES, ER, GP, AT, AR, AS, AZ,
+    GW, GA, RS, FT, TA, PM, CG, CGR, CGS, CGD, CGT, CGZ, CGF, GR, GRR, GRF, ssem, rsem,
+):
+    d = lax.axis_index("dp")
+    t = lax.axis_index("tensor")
+    z = t // 2
+    c = t % 2
+    sib = 2 * z + 1 - c
+    count = [0]
+    pending = []
+
+    def send(src, dst, dd, tt):
+        i = count[0]
+        count[0] += 1
+        cp = pltpu.make_async_remote_copy(
+            src_ref=src, dst_ref=dst, send_sem=ssem.at[i], recv_sem=rsem.at[i], device_id=(dd, tt), device_id_type=MESH
+        )
+        cp.start()
+        pending.append(cp)
+        return cp
+
+    def zpeer(k):
+        return 2 * ((z + k) % 4) + c
+
+    def dpeer(k):
+        return (d + k) % 4
+
+    barrier = pltpu.get_barrier_semaphore()
+    for k in range(1, 8):
+        pl.semaphore_signal(barrier, 1, device_id=(d, (t + k) % 8), device_id_type=MESH)
+    for k in range(1, 4):
+        pl.semaphore_signal(barrier, 1, device_id=(dpeer(k), t), device_id_type=MESH)
+
+    WBLK[...] = mm(eye(32), reduce_weight[...], 1, 1).astype(bf16)
+    CB[:, 0:2304] = mm(eye(32), conv_weight[...], 1, 1).astype(bf16)
+    CB[:, 2304:3328] = expand_weight[...]
+    eighth = jnp.full((8, 128), 0.125, f32)
+    lane = lax.broadcasted_iota(jnp.int32, (32, 128), 1)
+    packed = jnp.zeros((32, 128), f32)
+    for n, gain in enumerate((gain_middle, gain_inner)):
+        column = mm(jnp.broadcast_to(gain[...], (8, 32)), eighth, 0, 0, HIGHEST)
+        high, rest = split(column)
+        rest = column - high.astype(f32)
+        mid, low = split(rest)
+        for m, part in enumerate((high, mid, low)):
+            packed = jnp.where(lane == 3 * n + m, part.astype(f32), packed)
+    CB[:, 3328:3456] = packed.astype(bf16)
+    CB[:, 3456:3584] = jnp.zeros((32, 128), bf16)
+    pl.semaphore_wait(barrier, 10)
+
+    w_cp = []
+    for k in range(1, 8):
+        s = (t + k) % 8
+        w_cp.append(send(WBLK.at[:, pl.ds(pl.multiple_of(256 * (s // 2), 256), 256)], WT.at[pl.ds(pl.multiple_of(32 * t, 32), 32)], d, s))
+    WT[pl.ds(pl.multiple_of(32 * t, 32), 32), :] = WBLK[:, pl.ds(pl.multiple_of(256 * z, 256), 256)]
+    quarter = CB.at[:, pl.ds(pl.multiple_of(896 * d, 128), 896)]
+    wq_cp = [send(quarter, WQ.at[z], d, zpeer(k)) for k in range(1, 4)]
+    WQ[z] = quarter[...]
+
+    go_rows = jnp.broadcast_to(gain_outer[...], (8, 128))
+    go = mm(go_rows, eighth, 0, 0, HIGHEST)[:, 0:1]
+    pos = position[...]
+    pos_pair = mm(eye(128, f32), jnp.concatenate([pos, pos], axis=0), 1, 1, HIGHEST)
+    x_cp = []
+    for k in (1, 2, 3, 0):
+        p = (z + k) % 4
+        cols = pl.ds(pl.multiple_of(1152 * p, 128), 1152)
+        x = features[:, cols].astype(f32) + pos_pair
+        PLC[:, cols] = x
+        m = jnp.mean(x, axis=0, keepdims=True)
+        x = x - m
+        q = jnp.sum(x * x, axis=0, keepdims=True)
+        x = (x * go).astype(bf16)
+        for par, lo in ((0, 0), (1, 512)):
+            XW[par, p] = x[:, lo : lo + 640]
+            ST[2 * p + par, 0:1, :] = m[:, lo : lo + 640]
+            ST[2 * p + par, 1:2, :] = q[:, lo : lo + 640]
+        x_cp.append(send(XW.at[1 - c, p], XK.at[p, pl.ds(pl.multiple_of(128 * c, 128), 128)], d, sib))
+        XK[p, pl.ds(pl.multiple_of(128 * c, 128), 128), :] = XW[c, p]
+
+    for cp in w_cp:
+        cp.wait_recv()
+    WC[...] = mm(eye(256), WT[...], 1, 1).astype(bf16)
+    mine = WC[pl.ds(pl.multiple_of(128 * c, 128), 128), :].astype(f32)
+    colsum = mm(go_rows, mine, 1, 0, HIGHEST)[0:1]
+    for n in range(8):
+        ST[n, 2:3, 0:256] = colsum
+    q_cp = []
+    for n, k in enumerate((1, 2, 3, 0)):
+        p = (z + k) % 4
+        x_cp[n].wait_recv()
+        QF[...] = mm(XK[p], WC[...], 0, 0)
+        part = QF[pl.ds(pl.multiple_of(64 * c, 64), 576), :]
+        if k == 0:
+            QO[...] = part
+        else:
+            QS[k - 1] = part.astype(bf16)
+            q_cp.append(send(QS.at[k - 1], QR.at[k - 1], d, zpeer(k)))
+    st_cp = [send(ST.at[(t + k) % 8], SR.at[t], d, (t + k) % 8) for k in range(1, 8)]
+    SR[t] = ST[t]
+
+    POOL[...] = pool_pair()
+    for p in range(4):
+        high, low = split(PLC[:, 1152 * p : 1152 * (p + 1)])
+        PP[t, 288 * p : 288 * (p + 1), :] = (mm(POOL[...], high, 1, 1) + mm(POOL[...], low, 1, 1)).astype(bf16)
+    pp_cp = [send(PP.at[t], PP.at[t], d, zpeer(k)) for k in range(1, 4)]
+    pps_cp = [send(PP.at[t], PP.at[t], d, sib)]
+
+    for cp in wq_cp:
+        cp.wait_recv()
+    wb_cp = [send(WQ, WB.at[c, d], dpeer(k), t) for k in range(1, 4)]
+    WB[c, d] = WQ[...]
+    for cp in wb_cp:
+        cp.wait_recv()
+    ws_cp = send(WB.at[c], WB.at[c], d, sib)
+    ws_cp.wait_recv()
+    for cc in range(2):
+        for zz in range(4):
+            for dd in range(4):
+                WF[32 * (2 * zz + cc) : 32 * (2 * zz + cc + 1), 896 * dd : 896 * (dd + 1)] = WB[cc, dd, zz]
+    lane = lax.broadcasted_iota(jnp.int32, (8, 128), 1)
+    row = lax.broadcasted_iota(jnp.int32, (8, 128), 0)
+    pick = jnp.where((lane >= 3 * row) & (lane < 3 * row + 3) & (row < 2), 1.0, 0.0).astype(bf16)
+    gains = mm(pick, WF[:, 3328:3456], 1, 1)
+    gm, gi = gains[0:1], gains[1:2]
+    MT[...] = mm(readout_weight[...], WF[:, 2304:3328], 1, 1).astype(bf16)
+
+    for cp in st_cp:
+        cp.wait_recv()
+    m_t = SR[:, 0, :]
+    q_t = SR[:, 1, :]
+    sums = SR[:, 2, 0:256]
+    mean = jnp.mean(m_t, axis=0, keepdims=True)
+    dm = m_t - mean
+    var = (jnp.sum(q_t, axis=0, keepdims=True) + 128.0 * jnp.sum(dm * dm, axis=0, keepdims=True)) * (1.0 / 1024.0)
+    rstd = lax.rsqrt(var + epsilon)
+    valid = pl.ds(pl.multiple_of(64 * c, 64), 576)
+    QF[...] = mm(dm, sums, 0, 0, HIGHEST)
+    total = QO[...] + QF[valid, :]
+    QF[...] = mm(jnp.broadcast_to(rstd, (8, 640)), jnp.full((8, 256), 0.125, f32), 0, 0, HIGHEST)
+    scale = QF[valid, :]
+    for cp in q_cp:
+        cp.wait_recv()
+    for k in range(3):
+        total += QR[k].astype(f32)
+    RED[...] = jnp.zeros((24, 32, 256), f32)
+    RED[:, 0:24, :] = (total * scale).reshape(24, 24, 256)
+
+    xm, rm = norm_rows(RED[...].reshape(768, 256))
+    zm = xm * gm
+    hidden = zm * jax.nn.sigmoid(zm)
+    XM[...], ZM[...], RM[...] = xm, zm, jnp.broadcast_to(rm, (768, 128))
+    HB[0:32, :] = jnp.zeros((32, 768), bf16)
+    HB[800:832, :] = jnp.zeros((32, 768), bf16)
+    HB[32:800, 0:256] = pltpu.roll(hidden, 1, 0).astype(bf16)
+    HB[32:800, 256:512] = hidden.astype(bf16)
+    HB[32:800, 512:768] = pltpu.roll(hidden, 767, 0).astype(bf16)
+    conv = mm(HB[0:768, :], WF[:, 0:768], 1, 1)
+    conv += mm(HB[32:800, :], WF[:, 768:1536], 1, 1)
+    conv += mm(HB[64:832, :], WF[:, 1536:2304], 1, 1)
+    xi, ri = norm_rows(conv)
+    zi = xi * gi
+    activated = (zi * jax.nn.sigmoid(zi)).astype(bf16)
+    XI[...], ZI[...], RI[...] = xi, zi, jnp.broadcast_to(ri, (768, 128))
+    pool = pool_wide()
+    ACT[t] = mm(pool, activated, 1, 0).astype(bf16)
+    a_cp = [send(ACT.at[t], ACT.at[t], d, zpeer(k)) for k in range(1, 4)]
+    as_cp = [send(ACT.at[t], ACT.at[t], d, sib)]
+
+    for k in range(1, 4):
+        pp_cp[k - 1].wait_recv()
+        slot = 2 * ((z + 4 - k) % 4) + c
+        pps_cp.append(send(PP.at[slot], PP.at[slot], d, sib))
+    for cp in pps_cp:
+        cp.wait_recv()
+    before = jnp.zeros((512, 1152), f32)
+    for q in range(4):
+        both = jnp.concatenate([PP[2 * q], PP[2 * q + 1]], axis=1)
+        before += mm(readout_weight[:, 256 * q : 256 * (q + 1)], both, 1, 1)
+    BEF[...] = before
+
+    for k in range(1, 4):
+        a_cp[k - 1].wait_recv()
+        slot = 2 * ((z + 4 - k) % 4) + c
+        as_cp.append(send(ACT.at[slot], ACT.at[slot], d, sib))
+    for cp in as_cp:
+        cp.wait_recv()
+    for n in range(8):
+        ACL[n] = (ACT[n].astype(f32) * slot_live[n].astype(f32)).astype(bf16)
+    act_live = ACL[...].reshape(1152, 256)
+    BEF[...] += mm(MT[...], act_live, 1, 1)
+
+    @pl.loop(0, 16)
+    def _(u):
+        rows = pl.ds(pl.multiple_of(32 * u, 32), 32)
+        b = BEF[rows, :]
+        below = 0.5 * (1.0 + lax.erf(b * 0.7071067811865476))
+        density = jnp.exp(-0.5 * b * b) * 0.3989422804014327
+        readout_o[rows, :] = (b * below).astype(bf16)
+        GBT[rows, :] = (cotangent[rows, :].astype(f32) * (below + b * density)).astype(bf16)
+
+    terms = mm(GBT[...], MT[...], 0, 0).astype(bf16).reshape(8, 144, 256)
+    for n in range(8):
+        AT[n % 2, n // 2] = terms[n]
+    at_cp = send(AT.at[1 - c], AR, d, sib)
+    for q in range(4):
+        block = mm(GBT[...], readout_weight[:, 256 * q : 256 * (q + 1)], 0, 0).astype(bf16)
+        TE[0, q] = block[:, 0:128]
+        TE[1, q] = block[:, 128:256]
+    at_cp.wait_recv()
+    az_cp = []
+    for k in (1, 2, 3):
+        p = (z + k) % 4
+        AS[k - 1] = (AT[c, p].astype(f32) + AR[p].astype(f32)).astype(bf16)
+        az_cp.append(send(AS.at[k - 1], AZ.at[k - 1], d, zpeer(k)))
+    te_cp = send(TE.at[1 - c], TR, d, sib)
+    grad_act = AT[c, z].astype(f32) + AR[z].astype(f32)
+    for q in range(4):
+        both = jnp.concatenate([PP[2 * q], PP[2 * q + 1]], axis=1).astype(f32)
+        POOLED[:, 256 * q : 256 * (q + 1)] = (both + mm(act_live, WF[:, 2304 + 256 * q : 2560 + 256 * q], 1, 0)).astype(bf16)
+    for q in range(4):
+        GR[q] = mm(GBT[128 * q : 128 * (q + 1), :], POOLED[...], 1, 0).astype(bf16)
+    gr_cp = [send(GR.at[(d + k) % 4], GRR.at[d], dpeer(k), t) for k in range(1, 4)]
+    GRR[d] = GR[d]
+    te_cp.wait_recv()
+    es_cp = []
+    for k in (1, 2, 3):
+        p = (z + k) % 4
+        ES[k - 1] = (TE[c, p].astype(f32) + TR[p].astype(f32)).astype(bf16)
+        es_cp.append(send(ES.at[k - 1], ER.at[k - 1], d, zpeer(k)))
+    GP[...] = TE[c, z].astype(f32) + TR[z].astype(f32)
+
+    for cp in az_cp:
+        cp.wait_recv()
+    for k in range(3):
+        grad_act += AZ[k].astype(f32)
+    high, low = split(grad_act * slot_live[t].astype(f32))
+    grad_rows = mm(pool, high, 0, 0) + mm(pool, low, 0, 0)
+    zi = ZI[...]
+    gate = jax.nn.sigmoid(zi)
+    dy = grad_rows * (gate * (1.0 + zi * (1.0 - gate)))
+    xi = XI[...]
+    dyx_inner = dy * xi
+    gc = norm_rows_back(dy * gi, xi, RI[:, 0:1]).astype(bf16)
+    GB[0:32, :] = jnp.zeros((32, 256), bf16)
+    GB[800:832, :] = jnp.zeros((32, 256), bf16)
+    GB[32:800, :] = gc
+    back = mm(GB[64:832, :], WF[:, 0:768], 1, 0)
+    back += mm(GB[32:800, :], WF[:, 768:1536], 1, 0)
+    back += mm(GB[0:768, :], WF[:, 1536:2304], 1, 0)
+    grad_hidden = pltpu.roll(back[:, 0:256], 767, 0) + back[:, 256:512] + pltpu.roll(back[:, 512:768], 1, 0)
+    zm = ZM[...]
+    gate = jax.nn.sigmoid(zm)
+    inside = (lax.broadcasted_iota(jnp.int32, (768, 256), 0) & 31) < 24
+    dy = jnp.where(inside, grad_hidden * (gate * (1.0 + zm * (1.0 - gate))), 0.0)
+    xm = XM[...]
+    dyx_middle = dy * xm
+    gr = norm_rows_back(dy * gm, xm, RM[:, 0:1]).reshape(24, 32, 256)[:, 0:24, :].reshape(576, 256).astype(bf16)
+    GA[t] = gr
+    ga_cp = [send(GA.at[t], GA.at[t], d, zpeer(k)) for k in range(1, 4)]
+    gas_cp = [send(GA.at[t], GA.at[t], d, sib)]
+    QF[...] = jnp.zeros((640, 256), f32)
+    QF[valid, :] = gr.astype(f32)
+    wg = jnp.sum(sums, axis=0, keepdims=True)
+    s1 = mm(jnp.broadcast_to(wg, (8, 256)), QF[...], 1, 1, HIGHEST)[0:1]
+    QF[valid, :] = gr.astype(f32) * RED[:, 0:24, :].reshape(576, 256)
+    s2 = mm(jnp.ones((8, 256), f32), QF[...], 1, 1, HIGHEST)[0:1]
+    RS[t, 0:1, :] = mean
+    RS[t, 1:2, :] = rstd
+    RS[t, 2:3, :] = s1 * (1.0 / 1024.0)
+    RS[t, 3:4, :] = s2 * (1.0 / 1024.0)
+    rs_cp = [send(RS.at[t], RS.at[t], d, (t + k) % 8) for k in range(1, 8)]
+
+    def put(lo, value):
+        value = value.astype(bf16)
+        for n in range(8):
+            CG[n % 2, n // 2, :, lo : lo + value.shape[1]] = value[32 * n : 32 * (n + 1)]
+
+    for a in range(3):
+        put(768 * a, mm(gc, HB[32 * a : 32 * a + 768, :], 0, 0))
+    ones = jnp.ones((768, 128), bf16)
+    for lo, value in ((2304, dyx_inner), (2432, dyx_middle)):
+        high, low = split(value)
+        put(lo, mm(high, ones, 0, 0) + mm(low, ones, 0, 0))
+    cg_cp = send(CG.at[1 - c], CGR, d, sib)
+
+    for cp in gr_cp:
+        cp.wait_recv()
+    total = GRR[0].astype(f32)
+    for n in range(1, 4):
+        total += GRR[n].astype(f32)
+    GRF[d] = total.astype(bf16)
+    grf_cp = [send(GRF.at[d], GRF.at[d], dpeer(k), t) for k in range(1, 4)]
+
+    cg_cp.wait_recv()
+    CGS[...] = (CG[c].astype(f32) + CGR[...].astype(f32)).astype(bf16)
+    cgd_cp = []
+    for k in range(1, 4):
+        dd = dpeer(k)
+        cgd_cp.append(send(CGS.at[:, :, pl.ds(pl.multiple_of(640 * dd, 128), 640)], CGD.at[d], dd, t))
+    CGD[d] = CGS[:, :, pl.ds(pl.multiple_of(640 * d, 128), 640)]
+
+    for k in range(1, 4):
+        ga_cp[k - 1].wait_recv()
+        slot = 2 * ((z + 4 - k) % 4) + c
+        gas_cp.append(send(GA.at[slot], GA.at[slot], d, sib))
+    for cp in cgd_cp:
+        cp.wait_recv()
+    total = CGD[0].astype(f32)
+    for n in range(1, 4):
+        total += CGD[n].astype(f32)
+    CGT[...] = total.astype(bf16)
+    cgz_cp = [send(CGT.at[(z + k) % 4], CGZ.at[z], d, zpeer(k)) for k in range(1, 4)]
+    CGZ[z] = CGT[z]
+    for cp in es_cp:
+        cp.wait_recv()
+    gp = GP[...]
+    for k in range(3):
+        gp += ER[k].astype(f32)
+    gp_high, gp_low = split(gp)
+    FT[0] = mm(act_live, gp_high, 0, 0).astype(bf16)
+    for cp in cgz_cp:
+        cp.wait_recv()
+    total = CGZ[0].astype(f32)
+    for n in range(1, 4):
+        total += CGZ[n].astype(f32)
+    CGF[d] = total.astype(bf16)
+    cgf_cp = [send(CGF.at[d], CGF.at[d], dpeer(k), t) for k in range(1, 4)]
+    for cp in rs_cp:
+        cp.wait_recv()
+    for cp in gas_cp:
+        cp.wait_recv()
+    w_own = WC[pl.ds(pl.multiple_of(128 * c, 128), 128), :]
+    lane = lax.broadcasted_iota(jnp.int32, (4, 128), 1)
+    place_sum = jnp.zeros((128, 1152), f32)
+    gain_sum = jnp.zeros((128, 1), f32)
+    grad_reduce = jnp.zeros((128, 256), f32)
+    for p in range(4):
+        cols = slice(1152 * p, 1152 * (p + 1))
+        even, odd = RS[2 * p], RS[2 * p + 1]
+        stats = jnp.concatenate([even[:, 0:512], jnp.where(lane < 64, even[:, 512:640], odd[:, 0:128]), odd[:, 128:640]], axis=1)
+        g = GA[2 * p : 2 * p + 2].reshape(1152, 256)
+        gn = mm(w_own, g, 1, 1)
+        xhat = (PLC[:, cols] - stats[0:1]) * stats[1:2]
+        gain_sum += jnp.sum(gn * xhat, axis=1, keepdims=True)
+        grad_reduce += mm((xhat * go).astype(bf16), g, 1, 0)
+        spread = mm(gp_high[288 * p : 288 * (p + 1)], POOL[...], 0, 0) + mm(gp_low[288 * p : 288 * (p + 1)], POOL[...], 0, 0)
+        out = spread + stats[1:2] * (gn * go - stats[2:3] - xhat * stats[3:4])
+        gfeat_o[:, cols] = out
+        place_sum += out
+    FT[1] = jnp.transpose(grad_reduce).astype(bf16)
+    ft_cp = []
+    for k in range(1, 8):
+        s = (t + k) % 8
+        ft_cp.append(send(FT.at[:, pl.ds(pl.multiple_of(32 * s, 32), 32)], TA.at[d, t], d, s))
+    TA[d, t] = FT[:, pl.ds(pl.multiple_of(32 * t, 32), 32), :]
+    odd = pltpu.roll(place_sum, 576, 1)
+    lane = lax.broadcasted_iota(jnp.int32, (128, 640), 1)
+    PM[d] = jnp.where(lane < 576, place_sum[:, 0:640] + odd[:, 0:640], jnp.broadcast_to(gain_sum, (128, 640))).astype(bf16)
+    pm_cp = [send(PM.at[d], PM.at[d], dpeer(k), t) for k in range(1, 4)]
+    for cp in ft_cp:
+        cp.wait_recv()
+    ta_cp = [send(TA.at[d], TA.at[d], dpeer(k), t) for k in range(1, 4)]
+
+    for cp in grf_cp:
+        cp.wait_recv()
+    for q in range(4):
+        gread_o[128 * q : 128 * (q + 1), :] = GRF[q].astype(f32)
+    for cp in cgf_cp:
+        cp.wait_recv()
+    for q in range(4):
+        gconv_o[:, 640 * q : 640 * (q + 1)] = CGF[q].astype(f32)
+    for cp in pm_cp:
+        cp.wait_recv()
+    total = PM[0].astype(f32)
+    for n in range(1, 4):
+        total += PM[n].astype(f32)
+    gpos_o[...] = jnp.transpose(total)
+    for cp in ta_cp:
+        cp.wait_recv()
+    for s in range(8):
+        total = TA[0, s].astype(f32)
+        for n in range(1, 4):
+            total += TA[n, s].astype(f32)
+        gexp_o[:, 128 * s : 128 * (s + 1)] = total[0]
+        gred_o[:, 128 * s : 128 * (s + 1)] = total[1]
+    for cp in pending:
+        cp.wait_send()
+
+
+SCRATCH = (
+    ("WBLK", (32, 1024), bf16), ("WT", (256, 256), bf16), ("WC", (256, 256), bf16), ("CB", (32, 3584), bf16),
+    ("WQ", (4, 32, 896), bf16), ("WB", (2, 4, 4, 32, 896), bf16), ("WF", (256, 3584), bf16), ("MT", (512, 256), bf16),
+    ("POOL", (288, 1152), bf16), ("PLC", (128, 4608), f32), ("XW", (2, 4, 128, 640), bf16), ("XK", (4, 256, 640), bf16),
+    ("ST", (8, 4, 640), f32), ("SR", (8, 4, 640), f32), ("QF", (640, 256), f32), ("QS", (3, 576, 256), bf16),
+    ("QO", (576, 256), f32), ("QR", (3, 576, 256), bf16), ("RED", (24, 32, 256), f32), ("HB", (832, 768), bf16),
+    ("GB", (832, 256), bf16), ("XM", (768, 256), f32), ("ZM", (768, 256), f32), ("RM", (768, 128), f32),
+    ("XI", (768, 256), f32), ("ZI", (768, 256), f32), ("RI", (768, 128), f32), ("ACT", (8, 144, 256), bf16), ("ACL", (8, 144, 256), bf16),
+    ("PP", (8, 1152, 128), bf16), ("POOLED", (1152, 1024), bf16), ("BEF", (512, 1152), f32), ("GBT", (512, 1152), bf16),
+    ("TE", (2, 4, 1152, 128), bf16), ("TR", (4, 1152, 128), bf16), ("ES", (3, 1152, 128), bf16), ("ER", (3, 1152, 128), bf16),
+    ("GP", (1152, 128), f32), ("AT", (2, 4, 144, 256), bf16), ("AR", (4, 144, 256), bf16), ("AS", (3, 144, 256), bf16),
+    ("AZ", (3, 144, 256), bf16), ("GW", (8, 128), f32), ("GA", (8, 576, 256), bf16), ("RS", (8, 4, 640), f32),
+    ("FT", (2, 256, 128), bf16), ("TA", (4, 8, 2, 32, 128), bf16), ("PM", (4, 128, 640), bf16),
+    ("CG", (2, 4, 32, 2560), bf16), ("CGR", (4, 32, 2560), bf16), ("CGS", (4, 32, 2560), bf16), ("CGD", (4, 4, 32, 640), bf16),
+    ("CGT", (4, 32, 640), bf16), ("CGZ", (4, 32, 640), bf16), ("CGF", (4, 32, 640), bf16), ("GR", (4, 128, 1024), bf16), ("GRR", (4, 128, 1024), bf16),
+    ("GRF", (4, 128, 1024), bf16),
+)
+
+
+def local_by_image(features, slot_live, position, gain_outer, reduce_weight, gain_middle, conv_weight, gain_inner, expand_weight, readout_weight, cotangent):
+    vmem = pl.BlockSpec(memory_space=pltpu.VMEM)
+    smem = pl.BlockSpec(memory_space=pltpu.SMEM)
+    readout, gfeat, gpos, gexp, gred, gconv, gread = pl.pallas_call(
+        kernel,
+        out_shape=(
+            jax.ShapeDtypeStruct((512, 1152), bf16), jax.ShapeDtypeStruct((128, 4608), f32), jax.ShapeDtypeStruct((640, 128), f32),
+            jax.ShapeDtypeStruct((32, 1024), f32), jax.ShapeDtypeStruct((32, 1024), f32), jax.ShapeDtypeStruct((32, 2560), f32),
+            jax.ShapeDtypeStruct((512, 1024), f32),
+        ),
+        in_specs=[vmem, smem] + [vmem] * 9,
+        out_specs=[vmem] * 7,
+        scratch_shapes=[pltpu.VMEM(shape, dtype) for _, shape, dtype in SCRATCH]
+        + [pltpu.SemaphoreType.DMA((COPIES,)), pltpu.SemaphoreType.DMA((COPIES,))],
+        compiler_params=pltpu.CompilerParams(collective_id=0, has_side_effects=True, vmem_limit_bytes=63 * 2**20),
+    )(
+        features, slot_live, position.reshape(576, 128), gain_outer.reshape(1, 128), reduce_weight, gain_middle.reshape(1, 32),
+        conv_weight.reshape(2304, 32), gain_inner.reshape(1, 32), expand_weight, readout_weight, cotangent,
+    )
+    return (
+        readout, gfeat, gpos[0:576].reshape(24, 24, 128), gpos[576], gred.T, gconv[:, 2432],
+        gconv[:, 0:2304].T.reshape(3, 3, 256, 32), gconv[:, 2304], gexp, gread,
+    )
 
 
 def row_totals(leading, trailing):
@@ -56,7 +540,7 @@
     ].reshape(images * grid_side * grid_side, breadth)
 
 
-def local(
+def local_by_hidden(
     features,
     slot_live,
     position,
@@ -203,33 +687,14 @@
 
 
 def solution(mesh):
-    return jax.shard_map(
-        local,
-        mesh=mesh,
-        in_specs=(
-            P("tensor", "dp"),
-            P("dp"),
-            P(None, None, "tensor"),
-            P("tensor"),
-            P(None, "tensor"),
-            P("tensor"),
-            P(None, None, None, "tensor"),
-            P("tensor"),
-            P("tensor", None),
-            P("tensor", None),
-            P("tensor", "dp"),
-        ),
-        out_specs=(
-            P("tensor", "dp"),
-            P("tensor", "dp"),
-            P(None, None, "tensor"),
-            P("tensor"),
-            P(None, "tensor"),
-            P("tensor"),
-            P(None, None, None, "tensor"),
-            P("tensor"),
-            P("tensor", None),
-            P("tensor", None),
-        ),
-        check_vma=False,
-    )
+    parts, groups = mesh.shape["tensor"], mesh.shape["dp"]
+    specs = (P("tensor", "dp"), P("dp"), P(None, None, "tensor"), P("tensor"), P(None, "tensor"), P("tensor"), P(None, None, None, "tensor"), P("tensor"), P("tensor", None), P("tensor", None), P("tensor", "dp"))
+
+    def whole(*arrays):
+        by_image = (parts, groups) == (8, 4) and arrays[1].shape[0] == parts * groups
+        return jax.shard_map(
+            local_by_image if by_image else local_by_hidden, mesh=mesh, in_specs=specs,
+            out_specs=(P("tensor", "dp"), P("tensor", "dp"), *specs[2:10]), check_vma=False,
+        )(*arrays)
+
+    return whole

time: 1120 us -> 188 us (0.17)
  waiting for transfers between devices: 735 us -> 0 us
  blocking collectives: 177 us -> 0 us
  Pallas kernels: 0 us -> 171 us
  matrix products: 87.4 us -> 0 us
  other arithmetic: 55 us -> 0 us
  local copies, waits for them, and re-layouts: 42.4 us -> 16.4 us
  between operations: 15.1 us -> 0.67 us
    reduce_scatter x4 -> x0, waiting for transfers between devices: 456 us -> none  [the longest x1 185 us: local(): lax.psum_scatter(expand_terms, 'tensor', scatter_dimension=1, tiled=True)]
    all_gather x4 -> x0, waiting for transfers between devices: 236 us -> none  [the longest x1 89.6 us: local(): grad_full = lax.all_gather(grad_branch, 'tensor', axis=1, tiled=True)]
    psum x7 -> x0, blocking collectives: 177 us -> none  [the longest x6 167 us: row_totals(): return lax.psum((leading, trailing), 'tensor')]
    pallas_call x0 -> x1, Pallas kernels: none -> 171 us  [local_by_image(): pl.pallas_call(kernel, out_shape=(jax.ShapeDtypeStruct((512, 1152), bf16)...]
    dot_general x36 -> x0, matrix products: 87.4 us -> none  [the longest x9 19.8 us: local(): jnp.dot(grad_conv_low, conv_weight[shift_down, shift_across].T, preferred...]
    psum x1 -> x0, waiting for transfers between devices: 42.5 us -> none  [local(): lax.psum(grad_place.astype(jnp.bfloat16), 'dp').astype(jnp.float32)]
    add x4 -> x0, other arithmetic: 23.9 us -> none  [the longest x2 13.8 us: local(): grad_padded + jnp.pad(tap_back.reshape(images, grid_side, grid_side, hidd...]
    convert_element_type x16 -> x0, other arithmetic: 15.9 us -> none  [the longest x1 2.84 us: local(): lax.psum(grad_readout.astype(jnp.bfloat16), 'dp').astype(jnp.float32)]
  transfers between devices with their start and end apart: 9 -> 0, of which waited for: 9 -> 0; matrix products, arithmetic and copies ran while one was open for 3% -> 0% of each run, Pallas kernels for 0% -> 0%
where the time goes in v2:
time: 188 us
  Pallas kernels  171 us (91%)
  local copies, waits for them, and re-layouts  16.4 us (9%)
    pallas_call x1, Pallas kernels, local_by_image(): pl.pallas_call(kernel, out_shape=(jax.ShapeDtypeStruct((512, 1152), bf16)...  171 us
    unnamed x16, local copies, waits for them, and re-layouts  10.8 us

profile of v2, /device:TPU:0, one launch (start us, length us, event | category | flops | bytes accessed | tf_op | source)
XLA Modules:
  0.0 187.7 jit_solution(12301306117440581387)
XLA Ops:
  0.6 1.7 copy.25.reduce_weight
  2.3 2.0 %copy.24 = bf16[3,3,256,32]{3,2,1,0:T(8,128)(2,1)} copy(bf16[3,3,256,32]{2,3,1,0:T(8,128)(2,1)} %param.17) | data formatting | bytes 294912 | tf_op args[6]
  4.3 170.7 %shard_map.186 = (bf16[512,1152]{1,0:T(8,128)(2,1)}, f32[128,4608]{1,0:T(8,128)}, f32[640,128]{1,0:T(8,128)}, f32[32,1024]{1,0:T(8,128)}, f32[32,1024]{1,0:T(8,1...) custom-call(bf16[128,4608]{1,0:T(8,128)(2,1)} %features.1, s32[8]{0:T(128)} %slot_live.1, f32[576,128]{1,0:T(8,128)} %bitcast.14, ...), custom_call_target="tpu_custom_call" | custom-call | tf_op jit(solution)/shard_map/pallas_call | solution.py:471
  175.0 1.2 slice_bitcast_fusion.1
  176.2 1.7 slice.15
  177.9 1.4 slice_reduce_fusion
  179.2 0.0 copy-start
  179.2 1.1 slice_bitcast_fusion
  180.4 0.2 reshape.47
  180.5 0.8 copy.26
  181.3 2.4 %copy.32 = bf16[512,1152]{1,0:T(8,128)(2,1)} copy(bf16[512,1152]{1,0:T(8,128)(2,1)} %get-tuple-element.56) | data formatting | bytes 2359296
  183.7 0.0 copy-done
  183.7 0.0 copy-start.3
  183.7 0.0 copy-start.2
  183.7 0.0 copy-start.1
  183.7 1.4 copy.33
  185.1 0.0 copy-done.3
  185.1 0.7 copy.34
  185.7 0.0 copy-done.2
  185.7 0.7 copy.35
  186.4 0.0 copy-done.1
  186.4 1.3 copy.36
Async XLA Ops:
  179.2 4.4 %copy-start = (f32[128,4608]{1,0:T(8,128)S(1)}, f32[128,4608]{1,0:T(8,128)}, u32[]{:S(2)}) copy-start(f32[128,4608]{1,0:T(8,128)} %get-tuple-element.57) | copy-start | bytes 7077892
  183.7 1.4 copy-start.3
  183.7 2.1 %copy-start.2 = (f32[32,1024]{1,0:T(8,128)S(1)}, f32[32,1024]{1,0:T(8,128)}, u32[]{:S(2)}) copy-start(f32[32,1024]{1,0:T(8,128)} %get-tuple-element.64) | copy-start | bytes 393220
  183.7 2.7 %copy-start.1 = (f32[512,1024]{1,0:T(8,128)S(1)}, f32[512,1024]{1,0:T(8,128)}, u32[]{:S(2)}) copy-start(f32[512,1024]{1,0:T(8,128)} %get-tuple-element.65) | copy-start | bytes 6291460

commit v3 on v2

--- a/solution.py
+++ b/solution.py
@@ -8,7 +8,7 @@
 epsilon = 1e-05
 bf16 = jnp.bfloat16
 f32 = jnp.float32
-COPIES = 112
+COPIES = 160
 
 MESH = pl.DeviceIdType.MESH
 HIGHEST = lax.Precision.HIGHEST
@@ -64,18 +64,126 @@
     z = t // 2
     c = t % 2
     sib = 2 * z + 1 - c
-    count = [0]
+    side = z // 2
+    is_mid = ((z + 1) // 2) % 2
+    near_end, near_mid, far_end, far_mid = 3 * side, 1 + side, 3 - 3 * side, 2 - side
+    partner = z + 1 - 2 * (z % 2)
+    sends, arrivals = [0], [0]
     pending = []
 
+    def copy(src, dst, dd, tt, arrival):
+        cp = pltpu.make_async_remote_copy(
+            src_ref=src, dst_ref=dst, send_sem=ssem.at[sends[0]], recv_sem=rsem.at[arrival], device_id=(dd, tt), device_id_type=MESH
+        )
+        sends[0] += 1
+        return cp
+
+    def take(n):
+        arrivals[0] += n
+        return arrivals[0] - n
+
     def send(src, dst, dd, tt):
-        i = count[0]
-        count[0] += 1
-        cp = pltpu.make_async_remote_copy(
-            src_ref=src, dst_ref=dst, send_sem=ssem.at[i], recv_sem=rsem.at[i], device_id=(dd, tt), device_id_type=MESH
-        )
+        cp = copy(src, dst, dd, tt, take(1))
         cp.start()
         pending.append(cp)
         return cp
+
+    class Gather:
+        def __init__(self, buf, parts):
+            self.buf, self.parts, self.rows = buf, parts, buf.shape[1] // parts
+            self.base = take(4 * parts)
+            self.forwards = []
+
+        def view(self, zz, h):
+            return self.buf.at[2 * zz + c, pl.ds(h * self.rows, self.rows)]
+
+        def to(self, block, zz, h):
+            return copy(self.view(block, h), self.view(block, h), d, 2 * zz + c, self.base + 4 * h + block)
+
+        def start(self):
+            for zz in (far_mid, partner):
+                for h in range(self.parts):
+                    cp = self.to(z, zz, h)
+                    cp.start()
+                    pending.append(cp)
+            self.siblings = [send(self.buf.at[t], self.buf.at[t], d, sib)]
+
+        def arrived(self, block, h):
+            view = self.view(block, h)
+            pltpu.make_async_remote_copy(
+                src_ref=view, dst_ref=view, send_sem=ssem.at[0], recv_sem=rsem.at[self.base + 4 * h + block],
+                device_id=(d, sib), device_id_type=MESH,
+            ).wait_recv()
+
+        def forward(self, block, h):
+            cp = self.to(block, near_end, h)
+            self.forwards.append(cp)
+
+            @pl.when(is_mid == 1)
+            def _():
+                self.arrived(block, h)
+                cp.start()
+
+        def finish(self):
+            for h in range(self.parts):
+
+                @pl.when(is_mid == 0)
+                def _(h=h):
+                    self.arrived(far_mid, h)
+                    self.arrived(far_end, h)
+
+                self.arrived(partner, h)
+            for zz in (far_mid, far_end, partner):
+                self.siblings.append(send(self.buf.at[2 * zz + c], self.buf.at[2 * zz + c], d, sib))
+            for cp in self.siblings:
+                cp.wait_recv()
+
+        def drain(self):
+            @pl.when(is_mid == 1)
+            def _():
+                for cp in self.forwards:
+                    cp.wait_send()
+
+    order = (
+        far_end + is_mid * (near_end - far_end),
+        far_mid + is_mid * (far_end - far_mid),
+        near_mid + is_mid * (far_mid - near_mid),
+    )
+
+    class Summed:
+        def __init__(self, out, arrive):
+            self.out, self.arrive = out, arrive
+            self.base = take(4)
+            to = (partner, near_mid + is_mid * (far_end - near_mid), near_mid + is_mid * (far_mid - near_mid))
+            slot = (2 * is_mid, 1 + 2 * is_mid, 2 + is_mid)
+            self.cps = [copy(out.at[n], arrive.at[slot[n]], d, 2 * to[n] + c, self.base + slot[n]) for n in range(3)]
+            pending.extend(self.cps)
+
+        def wait(self, n):
+            view = self.arrive.at[n]
+            pltpu.make_async_remote_copy(
+                src_ref=view, dst_ref=view, send_sem=ssem.at[0], recv_sem=rsem.at[self.base + n], device_id=(d, sib), device_id_type=MESH
+            ).wait_recv()
+
+        def start(self):
+            self.cps[0].start()
+
+            @pl.when(is_mid == 0)
+            def _():
+                self.cps[1].start()
+                self.cps[2].start()
+
+        def add(self, n):
+            @pl.when(is_mid == 1)
+            def _():
+                self.wait(n)
+                self.out[n + 1] = (self.out[n + 1].astype(f32) + self.arrive[n].astype(f32)).astype(bf16)
+                self.cps[n + 1].start()
+
+        def result(self, own):
+            self.wait(2)
+            self.wait(3)
+            return own + self.arrive[2].astype(f32) + self.arrive[3].astype(f32)
 
     def zpeer(k):
         return 2 * ((z + k) % 4) + c
@@ -120,8 +228,7 @@
     pos = position[...]
     pos_pair = mm(eye(128, f32), jnp.concatenate([pos, pos], axis=0), 1, 1, HIGHEST)
     x_cp = []
-    for k in (1, 2, 3, 0):
-        p = (z + k) % 4
+    for p in (*order, z):
         cols = pl.ds(pl.multiple_of(1152 * p, 128), 1152)
         x = features[:, cols].astype(f32) + pos_pair
         PLC[:, cols] = x
@@ -143,31 +250,33 @@
     colsum = mm(go_rows, mine, 1, 0, HIGHEST)[0:1]
     for n in range(8):
         ST[n, 2:3, 0:256] = colsum
-    q_cp = []
-    for n, k in enumerate((1, 2, 3, 0)):
-        p = (z + k) % 4
+    st_cp = [send(ST.at[(t + k) % 8], SR.at[t], d, (t + k) % 8) for k in range(1, 8)]
+    SR[t] = ST[t]
+    for n, p in enumerate((*order, z)):
         x_cp[n].wait_recv()
         QF[...] = mm(XK[p], WC[...], 0, 0)
         part = QF[pl.ds(pl.multiple_of(64 * c, 64), 576), :]
-        if k == 0:
+        if n == 3:
             QO[...] = part
         else:
-            QS[k - 1] = part.astype(bf16)
-            q_cp.append(send(QS.at[k - 1], QR.at[k - 1], d, zpeer(k)))
-    st_cp = [send(ST.at[(t + k) % 8], SR.at[t], d, (t + k) % 8) for k in range(1, 8)]
-    SR[t] = ST[t]
+            QS[n] = part.astype(bf16)
+    reduced_sum = Summed(QS, QR)
+    reduced_sum.start()
 
     POOL[...] = pool_pair()
     for p in range(4):
         high, low = split(PLC[:, 1152 * p : 1152 * (p + 1)])
         PP[t, 288 * p : 288 * (p + 1), :] = (mm(POOL[...], high, 1, 1) + mm(POOL[...], low, 1, 1)).astype(bf16)
-    pp_cp = [send(PP.at[t], PP.at[t], d, zpeer(k)) for k in range(1, 4)]
-    pps_cp = [send(PP.at[t], PP.at[t], d, sib)]
+    placed_gather = Gather(PP, 1)
+    placed_gather.start()
 
     for cp in wq_cp:
         cp.wait_recv()
     wb_cp = [send(WQ, WB.at[c, d], dpeer(k), t) for k in range(1, 4)]
     WB[c, d] = WQ[...]
+    reduced_sum.add(0)
+    placed_gather.forward(far_mid, 0)
+    reduced_sum.add(1)
     for cp in wb_cp:
         cp.wait_recv()
     ws_cp = send(WB.at[c], WB.at[c], d, sib)
@@ -197,10 +306,7 @@
     total = QO[...] + QF[valid, :]
     QF[...] = mm(jnp.broadcast_to(rstd, (8, 640)), jnp.full((8, 256), 0.125, f32), 0, 0, HIGHEST)
     scale = QF[valid, :]
-    for cp in q_cp:
-        cp.wait_recv()
-    for k in range(3):
-        total += QR[k].astype(f32)
+    total = reduced_sum.result(total)
     RED[...] = jnp.zeros((24, 32, 256), f32)
     RED[:, 0:24, :] = (total * scale).reshape(24, 24, 256)
 
@@ -225,12 +331,8 @@
     a_cp = [send(ACT.at[t], ACT.at[t], d, zpeer(k)) for k in range(1, 4)]
     as_cp = [send(ACT.at[t], ACT.at[t], d, sib)]
 
-    for k in range(1, 4):
-        pp_cp[k - 1].wait_recv()
-        slot = 2 * ((z + 4 - k) % 4) + c
-        pps_cp.append(send(PP.at[slot], PP.at[slot], d, sib))
-    for cp in pps_cp:
-        cp.wait_recv()
+    placed_gather.forward(far_end, 0)
+    placed_gather.finish()
     before = jnp.zeros((512, 1152), f32)
     for q in range(4):
         both = jnp.concatenate([PP[2 * q], PP[2 * q + 1]], axis=1)
@@ -281,17 +383,17 @@
     gr_cp = [send(GR.at[(d + k) % 4], GRR.at[d], dpeer(k), t) for k in range(1, 4)]
     GRR[d] = GR[d]
     te_cp.wait_recv()
-    es_cp = []
-    for k in (1, 2, 3):
-        p = (z + k) % 4
-        ES[k - 1] = (TE[c, p].astype(f32) + TR[p].astype(f32)).astype(bf16)
-        es_cp.append(send(ES.at[k - 1], ER.at[k - 1], d, zpeer(k)))
+    for n, p in enumerate(order):
+        ES[n] = (TE[c, p].astype(f32) + TR[p].astype(f32)).astype(bf16)
+    pooled_sum = Summed(ES, ER)
+    pooled_sum.start()
     GP[...] = TE[c, z].astype(f32) + TR[z].astype(f32)
 
     for cp in az_cp:
         cp.wait_recv()
     for k in range(3):
         grad_act += AZ[k].astype(f32)
+    pooled_sum.add(0)
     high, low = split(grad_act * slot_live[t].astype(f32))
     grad_rows = mm(pool, high, 0, 0) + mm(pool, low, 0, 0)
     zi = ZI[...]
@@ -315,8 +417,9 @@
     dyx_middle = dy * xm
     gr = norm_rows_back(dy * gm, xm, RM[:, 0:1]).reshape(24, 32, 256)[:, 0:24, :].reshape(576, 256).astype(bf16)
     GA[t] = gr
-    ga_cp = [send(GA.at[t], GA.at[t], d, zpeer(k)) for k in range(1, 4)]
-    gas_cp = [send(GA.at[t], GA.at[t], d, sib)]
+    grad_gather = Gather(GA, 2)
+    grad_gather.start()
+    pooled_sum.add(1)
     QF[...] = jnp.zeros((640, 256), f32)
     QF[valid, :] = gr.astype(f32)
     wg = jnp.sum(sums, axis=0, keepdims=True)
@@ -358,10 +461,10 @@
         cgd_cp.append(send(CGS.at[:, :, pl.ds(pl.multiple_of(640 * dd, 128), 640)], CGD.at[d], dd, t))
     CGD[d] = CGS[:, :, pl.ds(pl.multiple_of(640 * d, 128), 640)]
 
-    for k in range(1, 4):
-        ga_cp[k - 1].wait_recv()
-        slot = 2 * ((z + 4 - k) % 4) + c
-        gas_cp.append(send(GA.at[slot], GA.at[slot], d, sib))
+    for h in range(2):
+        grad_gather.forward(far_mid, h)
+    for h in range(2):
+        grad_gather.forward(far_end, h)
     for cp in cgd_cp:
         cp.wait_recv()
     total = CGD[0].astype(f32)
@@ -370,11 +473,7 @@
     CGT[...] = total.astype(bf16)
     cgz_cp = [send(CGT.at[(z + k) % 4], CGZ.at[z], d, zpeer(k)) for k in range(1, 4)]
     CGZ[z] = CGT[z]
-    for cp in es_cp:
-        cp.wait_recv()
-    gp = GP[...]
-    for k in range(3):
-        gp += ER[k].astype(f32)
+    gp = pooled_sum.result(GP[...])
     gp_high, gp_low = split(gp)
     FT[0] = mm(act_live, gp_high, 0, 0).astype(bf16)
     for cp in cgz_cp:
@@ -386,8 +485,7 @@
     cgf_cp = [send(CGF.at[d], CGF.at[d], dpeer(k), t) for k in range(1, 4)]
     for cp in rs_cp:
         cp.wait_recv()
-    for cp in gas_cp:
-        cp.wait_recv()
+    grad_gather.finish()
     w_own = WC[pl.ds(pl.multiple_of(128 * c, 128), 128), :]
     lane = lax.broadcasted_iota(jnp.int32, (4, 128), 1)
     place_sum = jnp.zeros((128, 1152), f32)
@@ -444,6 +542,8 @@
         gred_o[:, 128 * s : 128 * (s + 1)] = total[1]
     for cp in pending:
         cp.wait_send()
+    placed_gather.drain()
+    grad_gather.drain()
 
 
 SCRATCH = (
@@ -451,11 +551,11 @@
     ("WQ", (4, 32, 896), bf16), ("WB", (2, 4, 4, 32, 896), bf16), ("WF", (256, 3584), bf16), ("MT", (512, 256), bf16),
     ("POOL", (288, 1152), bf16), ("PLC", (128, 4608), f32), ("XW", (2, 4, 128, 640), bf16), ("XK", (4, 256, 640), bf16),
     ("ST", (8, 4, 640), f32), ("SR", (8, 4, 640), f32), ("QF", (640, 256), f32), ("QS", (3, 576, 256), bf16),
-    ("QO", (576, 256), f32), ("QR", (3, 576, 256), bf16), ("RED", (24, 32, 256), f32), ("HB", (832, 768), bf16),
+    ("QO", (576, 256), f32), ("QR", (4, 576, 256), bf16), ("RED", (24, 32, 256), f32), ("HB", (832, 768), bf16),
     ("GB", (832, 256), bf16), ("XM", (768, 256), f32), ("ZM", (768, 256), f32), ("RM", (768, 128), f32),
     ("XI", (768, 256), f32), ("ZI", (768, 256), f32), ("RI", (768, 128), f32), ("ACT", (8, 144, 256), bf16), ("ACL", (8, 144, 256), bf16),
     ("PP", (8, 1152, 128), bf16), ("POOLED", (1152, 1024), bf16), ("BEF", (512, 1152), f32), ("GBT", (512, 1152), bf16),
-    ("TE", (2, 4, 1152, 128), bf16), ("TR", (4, 1152, 128), bf16), ("ES", (3, 1152, 128), bf16), ("ER", (3, 1152, 128), bf16),
+    ("TE", (2, 4, 1152, 128), bf16), ("TR", (4, 1152, 128), bf16), ("ES", (3, 1152, 128), bf16), ("ER", (4, 1152, 128), bf16),
     ("GP", (1152, 128), f32), ("AT", (2, 4, 144, 256), bf16), ("AR", (4, 144, 256), bf16), ("AS", (3, 144, 256), bf16),
     ("AZ", (3, 144, 256), bf16), ("GW", (8, 128), f32), ("GA", (8, 576, 256), bf16), ("RS", (8, 4, 640), f32),
     ("FT", (2, 256, 128), bf16), ("TA", (4, 8, 2, 32, 128), bf16), ("PM", (4, 128, 640), bf16),

time: 188 us -> 160 us (0.85)
  Pallas kernels: 171 us -> 142 us
    pallas_call x1, Pallas kernels: 171 us -> 142 us  [local_by_image(): pl.pallas_call(kernel, out_shape=(jax.ShapeDtypeStruct((512, 1152), bf16)...]
where the time goes in v3:
time: 160 us; the launch traced here: 159 us
  Pallas kernels  142 us (89%)
  local copies, waits for them, and re-layouts  16.4 us (10%)
    pallas_call x1, Pallas kernels, local_by_image(): pl.pallas_call(kernel, out_shape=(jax.ShapeDtypeStruct((512, 1152), bf16)...  142 us
    unnamed x16, local copies, waits for them, and re-layouts  10.8 us

profile of v3, /device:TPU:0, one launch (start us, length us, event | category | flops | bytes accessed | tf_op | source)
XLA Modules:
  0.0 159.2 jit_solution(10270246218745919944)
XLA Ops:
  0.6 1.7 %copy.25.reduce_weight = bf16[1024,32]{1,0:T(8,128)(2,1)} copy(bf16[1024,32]{0,1:T(8,128)(2,1)} %param.15) | data formatting | bytes 131072 | tf_op args[4]
  2.3 2.0 %copy.24 = bf16[3,3,256,32]{3,2,1,0:T(8,128)(2,1)} copy(bf16[3,3,256,32]{2,3,1,0:T(8,128)(2,1)} %param.17) | data formatting | bytes 294912 | tf_op args[6]
  4.3 142.1 %shard_map.186 = (bf16[512,1152]{1,0:T(8,128)(2,1)}, f32[128,4608]{1,0:T(8,128)}, f32[640,128]{1,0:T(8,128)}, f32[32,1024]{1,0:T(8,128)}, f32[32,1024]{1,0:T(8,1...) custom-call(bf16[128,4608]{1,0:T(8,128)(2,1)} %features.1, s32[8]{0:T(128)} %slot_live.1, f32[576,128]{1,0:T(8,128)} %bitcast.14, ...), custom_call_target="tpu_custom_call" | custom-call | tf_op jit(solution)/shard_map/pallas_call | solution.py:571
  146.4 1.2 slice_bitcast_fusion.1
  147.6 1.7 %slice.15 = f32[576,128]{1,0:T(8,128)} slice(f32[640,128]{1,0:T(8,128)} %get-tuple-element.19), slice={[0:576], [0:128]} | slice | bytes 589824 | tf_op jit(solution)/shard_map/slice | solution.py:588
  149.3 1.4 slice_reduce_fusion
  150.7 0.0 copy-start
  150.7 1.1 slice_bitcast_fusion
  151.8 0.2 reshape.47
  152.0 0.8 copy.26
  152.7 2.4 %copy.32 = bf16[512,1152]{1,0:T(8,128)(2,1)} copy(bf16[512,1152]{1,0:T(8,128)(2,1)} %get-tuple-element.56) | data formatting | bytes 2359296
  155.1 0.0 copy-done
  155.1 0.0 copy-start.3
  155.1 0.0 copy-start.2
  155.1 0.0 copy-start.1
  155.1 1.4 copy.33
  156.5 0.0 copy-done.3
  156.5 0.7 copy.34
  157.2 0.0 copy-done.2
  157.2 0.7 copy.35
  157.9 0.0 copy-done.1
  157.9 1.3 copy.36
Async XLA Ops:
  150.7 4.4 %copy-start = (f32[128,4608]{1,0:T(8,128)S(1)}, f32[128,4608]{1,0:T(8,128)}, u32[]{:S(2)}) copy-start(f32[128,4608]{1,0:T(8,128)} %get-tuple-element.57) | copy-start | bytes 7077892
  155.1 1.4 copy-start.3
  155.1 2.1 %copy-start.2 = (f32[32,1024]{1,0:T(8,128)S(1)}, f32[32,1024]{1,0:T(8,128)}, u32[]{:S(2)}) copy-start(f32[32,1024]{1,0:T(8,128)} %get-tuple-element.64) | copy-start | bytes 393220
  155.1 2.7 %copy-start.1 = (f32[512,1024]{1,0:T(8,128)S(1)}, f32[512,1024]{1,0:T(8,128)}, u32[]{:S(2)}) copy-start(f32[512,1024]{1,0:T(8,128)} %get-tuple-element.65) | copy-start | bytes 6291460

commit v4 on v3

--- a/solution.py
+++ b/solution.py
@@ -53,11 +53,11 @@
 
 
 def kernel(
-    features, slot_live, position, gain_outer, reduce_weight, gain_middle, conv_weight, gain_inner, expand_weight, readout_weight, cotangent,
+    features, slot_live, position, gain_outer, reduce_weight, gain_middle, conv_weight, gain_inner, expand_weight, readout_h, cotangent_h,
     readout_o, gfeat_o, gpos_o, gexp_o, gred_o, gconv_o, gread_o,
-    WBLK, WT, WC, CB, WQ, WB, WF, MT, POOL, PLC, XW, XK, ST, SR, QF, QS, QO, QR, RED, HB, GB,
-    XM, ZM, RM, XI, ZI, RI, ACT, ACL, PP, POOLED, BEF, GBT, TE, TR, ES, ER, GP, AT, AR, AS, AZ,
-    GW, GA, RS, FT, TA, PM, CG, CGR, CGS, CGD, CGT, CGZ, CGF, GR, GRR, GRF, ssem, rsem,
+    readout_weight, cotangent, RO, GF, SP, WT, WC, CB, WQ, WB, WF, MT, POOL, PLC, XW, XK, ST, SR, QF, QS, QO, QR, RED, HB, GB,
+    XM, ZM, RM, XI, ZI, RI, ACT, ACL, PP, POOLED, BEF, GBT, GBR, TE, TR, ES, ER, GP, AT, AR, AS, AZ,
+    RSC, GA, RS, FT, TA, PM, PR, PF, CG, CGR, CGS, CGD, CGT, CGZ, CGF, GR, GRR, GRF, ssem, rsem, lsem,
 ):
     d = lax.axis_index("dp")
     t = lax.axis_index("tensor")
@@ -100,12 +100,13 @@
         def to(self, block, zz, h):
             return copy(self.view(block, h), self.view(block, h), d, 2 * zz + c, self.base + 4 * h + block)
 
-        def start(self):
-            for zz in (far_mid, partner):
-                for h in range(self.parts):
-                    cp = self.to(z, zz, h)
-                    cp.start()
-                    pending.append(cp)
+        def start(self, zz):
+            for h in range(self.parts):
+                cp = self.to(z, zz, h)
+                cp.start()
+                pending.append(cp)
+
+        def own(self):
             self.siblings = [send(self.buf.at[t], self.buf.at[t], d, sib)]
 
         def arrived(self, block, h):
@@ -124,19 +125,21 @@
                 self.arrived(block, h)
                 cp.start()
 
-        def finish(self):
-            for h in range(self.parts):
-
-                @pl.when(is_mid == 0)
-                def _(h=h):
-                    self.arrived(far_mid, h)
-                    self.arrived(far_end, h)
-
-                self.arrived(partner, h)
-            for zz in (far_mid, far_end, partner):
-                self.siblings.append(send(self.buf.at[2 * zz + c], self.buf.at[2 * zz + c], d, sib))
-            for cp in self.siblings:
-                cp.wait_recv()
+        def ready(self, n):
+            if n > 0:
+                block = (partner, far_mid, far_end)[n - 1]
+                for h in range(self.parts):
+                    if n == 1:
+                        self.arrived(block, h)
+                    else:
+
+                        @pl.when(is_mid == 0)
+                        def _(h=h):
+                            self.arrived(block, h)
+
+                slot = self.buf.at[2 * block + c]
+                self.siblings.append(send(slot, slot, d, sib))
+            self.siblings[n].wait_recv()
 
         def drain(self):
             @pl.when(is_mid == 1)
@@ -165,13 +168,14 @@
                 src_ref=view, dst_ref=view, send_sem=ssem.at[0], recv_sem=rsem.at[self.base + n], device_id=(d, sib), device_id_type=MESH
             ).wait_recv()
 
-        def start(self):
-            self.cps[0].start()
-
-            @pl.when(is_mid == 0)
-            def _():
-                self.cps[1].start()
-                self.cps[2].start()
+        def start(self, n):
+            if n == 0:
+                self.cps[0].start()
+            else:
+
+                @pl.when(is_mid == 0)
+                def _():
+                    self.cps[n].start()
 
         def add(self, n):
             @pl.when(is_mid == 1)
@@ -191,14 +195,27 @@
     def dpeer(k):
         return (d + k) % 4
 
+    operand_cp = [
+        pltpu.make_async_copy(readout_h, readout_weight, lsem.at[0]),
+        pltpu.make_async_copy(cotangent_h, cotangent, lsem.at[1]),
+    ]
+    for cp in operand_cp:
+        cp.start()
+    result_cp = []
+
+    def store(src, dst):
+        cp = pltpu.make_async_copy(src, dst, lsem.at[2 + len(result_cp)])
+        cp.start()
+        result_cp.append(cp)
+
     barrier = pltpu.get_barrier_semaphore()
     for k in range(1, 8):
         pl.semaphore_signal(barrier, 1, device_id=(d, (t + k) % 8), device_id_type=MESH)
     for k in range(1, 4):
         pl.semaphore_signal(barrier, 1, device_id=(dpeer(k), t), device_id_type=MESH)
 
-    WBLK[...] = mm(eye(32), reduce_weight[...], 1, 1).astype(bf16)
-    CB[:, 0:2304] = mm(eye(32), conv_weight[...], 1, 1).astype(bf16)
+    for n in range(9):
+        CB[:, 256 * n : 256 * (n + 1)] = conv_weight[n]
     CB[:, 2304:3328] = expand_weight[...]
     eighth = jnp.full((8, 128), 0.125, f32)
     lane = lax.broadcasted_iota(jnp.int32, (32, 128), 1)
@@ -212,16 +229,19 @@
             packed = jnp.where(lane == 3 * n + m, part.astype(f32), packed)
     CB[:, 3328:3456] = packed.astype(bf16)
     CB[:, 3456:3584] = jnp.zeros((32, 128), bf16)
+    POOL[...] = pool_pair()
     pl.semaphore_wait(barrier, 10)
 
     w_cp = []
     for k in range(1, 8):
         s = (t + k) % 8
-        w_cp.append(send(WBLK.at[:, pl.ds(pl.multiple_of(256 * (s // 2), 256), 256)], WT.at[pl.ds(pl.multiple_of(32 * t, 32), 32)], d, s))
-    WT[pl.ds(pl.multiple_of(32 * t, 32), 32), :] = WBLK[:, pl.ds(pl.multiple_of(256 * z, 256), 256)]
+        w_cp.append(send(reduce_weight.at[:, pl.ds(pl.multiple_of(256 * (s // 2), 256), 256)], WT.at[pl.ds(pl.multiple_of(32 * t, 32), 32)], d, s))
+    WT[pl.ds(pl.multiple_of(32 * t, 32), 32), :] = reduce_weight[:, pl.ds(pl.multiple_of(256 * z, 256), 256)]
     quarter = CB.at[:, pl.ds(pl.multiple_of(896 * d, 128), 896)]
     wq_cp = [send(quarter, WQ.at[z], d, zpeer(k)) for k in range(1, 4)]
     WQ[z] = quarter[...]
+    WB[c, d, z] = quarter[...]
+    wb_cp = [send(WQ.at[z], WB.at[c, d, z], dpeer(k), t) for k in range(1, 4)]
 
     go_rows = jnp.broadcast_to(gain_outer[...], (8, 128))
     go = mm(go_rows, eighth, 0, 0, HIGHEST)[:, 0:1]
@@ -252,6 +272,7 @@
         ST[n, 2:3, 0:256] = colsum
     st_cp = [send(ST.at[(t + k) % 8], SR.at[t], d, (t + k) % 8) for k in range(1, 8)]
     SR[t] = ST[t]
+    reduced_sum = Summed(QS, QR)
     for n, p in enumerate((*order, z)):
         x_cp[n].wait_recv()
         QF[...] = mm(XK[p], WC[...], 0, 0)
@@ -260,20 +281,21 @@
             QO[...] = part
         else:
             QS[n] = part.astype(bf16)
-    reduced_sum = Summed(QS, QR)
-    reduced_sum.start()
-
-    POOL[...] = pool_pair()
+            reduced_sum.start(n)
     for p in range(4):
         high, low = split(PLC[:, 1152 * p : 1152 * (p + 1)])
         PP[t, 288 * p : 288 * (p + 1), :] = (mm(POOL[...], high, 1, 1) + mm(POOL[...], low, 1, 1)).astype(bf16)
     placed_gather = Gather(PP, 1)
-    placed_gather.start()
-
-    for cp in wq_cp:
-        cp.wait_recv()
-    wb_cp = [send(WQ, WB.at[c, d], dpeer(k), t) for k in range(1, 4)]
-    WB[c, d] = WQ[...]
+    placed_gather.start(far_mid)
+    placed_gather.start(partner)
+    placed_gather.own()
+
+
+    for n in range(1, 4):
+        wq_cp[n - 1].wait_recv()
+        block = (z + 4 - n) % 4
+        wb_cp += [send(WQ.at[block], WB.at[c, d, block], dpeer(k), t) for k in range(1, 4)]
+        WB[c, d, block] = WQ[block]
     reduced_sum.add(0)
     placed_gather.forward(far_mid, 0)
     reduced_sum.add(1)
@@ -290,7 +312,6 @@
     pick = jnp.where((lane >= 3 * row) & (lane < 3 * row + 3) & (row < 2), 1.0, 0.0).astype(bf16)
     gains = mm(pick, WF[:, 3328:3456], 1, 1)
     gm, gi = gains[0:1], gains[1:2]
-    MT[...] = mm(readout_weight[...], WF[:, 2304:3328], 1, 1).astype(bf16)
 
     for cp in st_cp:
         cp.wait_recv()
@@ -332,17 +353,23 @@
     as_cp = [send(ACT.at[t], ACT.at[t], d, sib)]
 
     placed_gather.forward(far_end, 0)
-    placed_gather.finish()
-    before = jnp.zeros((512, 1152), f32)
-    for q in range(4):
+    for cp in operand_cp:
+        cp.wait()
+    MT[...] = mm(readout_weight[...], WF[:, 2304:3328], 1, 1).astype(bf16)
+    for n, q in enumerate((z, partner, far_mid, far_end)):
+        if n == 2:
+            for k in range(1, 4):
+                a_cp[k - 1].wait_recv()
+                slot = 2 * ((z + 4 - k) % 4) + c
+                as_cp.append(send(ACT.at[slot], ACT.at[slot], d, sib))
+        placed_gather.ready(n)
         both = jnp.concatenate([PP[2 * q], PP[2 * q + 1]], axis=1)
-        before += mm(readout_weight[:, 256 * q : 256 * (q + 1)], both, 1, 1)
-    BEF[...] = before
-
-    for k in range(1, 4):
-        a_cp[k - 1].wait_recv()
-        slot = 2 * ((z + 4 - k) % 4) + c
-        as_cp.append(send(ACT.at[slot], ACT.at[slot], d, sib))
+        part = mm(readout_weight[:, pl.ds(pl.multiple_of(256 * q, 256), 256)], both, 1, 1)
+        if n == 0:
+            BEF[...] = part
+        else:
+            BEF[...] += part
+
     for cp in as_cp:
         cp.wait_recv()
     for n in range(8):
@@ -354,27 +381,45 @@
     def _(u):
         rows = pl.ds(pl.multiple_of(32 * u, 32), 32)
         b = BEF[rows, :]
-        below = 0.5 * (1.0 + lax.erf(b * 0.7071067811865476))
-        density = jnp.exp(-0.5 * b * b) * 0.3989422804014327
-        readout_o[rows, :] = (b * below).astype(bf16)
+        bell = jnp.exp(-0.5 * b * b)
+        density = bell * 0.3989422804014327
+        u = 1.0 / (1.0 + 0.23164189 * jnp.abs(b))
+        beyond = u * (0.127414796 + u * (-0.142248368 + u * (0.7107068705 + u * (-0.7265760135 + u * 0.5307027145)))) * bell
+        below = jnp.where(b >= 0.0, 1.0 - beyond, beyond)
+        RO[rows, :] = (b * below).astype(bf16)
         GBT[rows, :] = (cotangent[rows, :].astype(f32) * (below + b * density)).astype(bf16)
 
-    terms = mm(GBT[...], MT[...], 0, 0).astype(bf16).reshape(8, 144, 256)
+    store(RO, readout_o)
+    GBR[...] = jnp.transpose(GBT[...])
+    terms = mm(GBR[...], MT[...], 1, 0).astype(bf16).reshape(8, 144, 256)
     for n in range(8):
         AT[n % 2, n // 2] = terms[n]
     at_cp = send(AT.at[1 - c], AR, d, sib)
-    for q in range(4):
-        block = mm(GBT[...], readout_weight[:, 256 * q : 256 * (q + 1)], 0, 0).astype(bf16)
+    pooled_sum = Summed(ES, ER)
+    te_cp = []
+
+    def pooled_block(n):
+        te_cp[n].wait_recv()
+        ES[n] = (TE[c, order[n]].astype(f32) + TR[order[n]].astype(f32)).astype(bf16)
+        pooled_sum.start(n)
+
+    for n, q in enumerate((*order, z)):
+        block = mm(GBR[...], readout_weight[:, pl.ds(pl.multiple_of(256 * q, 256), 256)], 1, 0).astype(bf16)
         TE[0, q] = block[:, 0:128]
         TE[1, q] = block[:, 128:256]
-    at_cp.wait_recv()
-    az_cp = []
-    for k in (1, 2, 3):
-        p = (z + k) % 4
-        AS[k - 1] = (AT[c, p].astype(f32) + AR[p].astype(f32)).astype(bf16)
-        az_cp.append(send(AS.at[k - 1], AZ.at[k - 1], d, zpeer(k)))
-    te_cp = send(TE.at[1 - c], TR, d, sib)
-    grad_act = AT[c, z].astype(f32) + AR[z].astype(f32)
+        te_cp.append(send(TE.at[1 - c, q], TR.at[q], d, sib))
+        if n == 0:
+            at_cp.wait_recv()
+            az_cp = []
+            for k in (1, 2, 3):
+                p = (z + k) % 4
+                AS[k - 1] = (AT[c, p].astype(f32) + AR[p].astype(f32)).astype(bf16)
+                az_cp.append(send(AS.at[k - 1], AZ.at[k - 1], d, zpeer(k)))
+            grad_act = AT[c, z].astype(f32) + AR[z].astype(f32)
+        else:
+            pooled_block(n - 1)
+    te_cp[3].wait_recv()
+    GP[...] = TE[c, z].astype(f32) + TR[z].astype(f32)
     for q in range(4):
         both = jnp.concatenate([PP[2 * q], PP[2 * q + 1]], axis=1).astype(f32)
         POOLED[:, 256 * q : 256 * (q + 1)] = (both + mm(act_live, WF[:, 2304 + 256 * q : 2560 + 256 * q], 1, 0)).astype(bf16)
@@ -382,12 +427,6 @@
         GR[q] = mm(GBT[128 * q : 128 * (q + 1), :], POOLED[...], 1, 0).astype(bf16)
     gr_cp = [send(GR.at[(d + k) % 4], GRR.at[d], dpeer(k), t) for k in range(1, 4)]
     GRR[d] = GR[d]
-    te_cp.wait_recv()
-    for n, p in enumerate(order):
-        ES[n] = (TE[c, p].astype(f32) + TR[p].astype(f32)).astype(bf16)
-    pooled_sum = Summed(ES, ER)
-    pooled_sum.start()
-    GP[...] = TE[c, z].astype(f32) + TR[z].astype(f32)
 
     for cp in az_cp:
         cp.wait_recv()
@@ -418,19 +457,23 @@
     gr = norm_rows_back(dy * gm, xm, RM[:, 0:1]).reshape(24, 32, 256)[:, 0:24, :].reshape(576, 256).astype(bf16)
     GA[t] = gr
     grad_gather = Gather(GA, 2)
-    grad_gather.start()
-    pooled_sum.add(1)
-    QF[...] = jnp.zeros((640, 256), f32)
-    QF[valid, :] = gr.astype(f32)
+    grad_gather.start(far_mid)
     wg = jnp.sum(sums, axis=0, keepdims=True)
-    s1 = mm(jnp.broadcast_to(wg, (8, 256)), QF[...], 1, 1, HIGHEST)[0:1]
-    QF[valid, :] = gr.astype(f32) * RED[:, 0:24, :].reshape(576, 256)
-    s2 = mm(jnp.ones((8, 256), f32), QF[...], 1, 1, HIGHEST)[0:1]
+    grad_rounded = gr.astype(f32)
+    s1 = jnp.sum(grad_rounded * wg, axis=1, keepdims=True)
+    s2 = jnp.sum(grad_rounded * RED[:, 0:24, :].reshape(576, 256), axis=1, keepdims=True)
+    lane = lax.broadcasted_iota(jnp.int32, (576, 128), 1)
+    RSC[0:64, :] = jnp.zeros((64, 128), f32)
+    RSC[576:640, :] = jnp.zeros((64, 128), f32)
+    RSC[valid, :] = jnp.where(lane == 0, s1, s2) * (1.0 / 1024.0)
+    row_sums = jnp.transpose(RSC[...])
     RS[t, 0:1, :] = mean
     RS[t, 1:2, :] = rstd
-    RS[t, 2:3, :] = s1 * (1.0 / 1024.0)
-    RS[t, 3:4, :] = s2 * (1.0 / 1024.0)
+    RS[t, 2:4, :] = row_sums[0:2]
     rs_cp = [send(RS.at[t], RS.at[t], d, (t + k) % 8) for k in range(1, 8)]
+    grad_gather.start(partner)
+    grad_gather.own()
+    pooled_sum.add(1)
 
     def put(lo, value):
         value = value.astype(bf16)
@@ -451,7 +494,6 @@
     for n in range(1, 4):
         total += GRR[n].astype(f32)
     GRF[d] = total.astype(bf16)
-    grf_cp = [send(GRF.at[d], GRF.at[d], dpeer(k), t) for k in range(1, 4)]
 
     cg_cp.wait_recv()
     CGS[...] = (CG[c].astype(f32) + CGR[...].astype(f32)).astype(bf16)
@@ -460,86 +502,110 @@
         dd = dpeer(k)
         cgd_cp.append(send(CGS.at[:, :, pl.ds(pl.multiple_of(640 * dd, 128), 640)], CGD.at[d], dd, t))
     CGD[d] = CGS[:, :, pl.ds(pl.multiple_of(640 * d, 128), 640)]
+    grf_cp = [send(GRF.at[d], GRF.at[d], dpeer(k), t) for k in range(1, 4)]
 
     for h in range(2):
         grad_gather.forward(far_mid, h)
-    for h in range(2):
-        grad_gather.forward(far_end, h)
-    for cp in cgd_cp:
-        cp.wait_recv()
-    total = CGD[0].astype(f32)
+    def turn(n):
+        for k in range(1, 8):
+            s = (t + k) % 8
+            yield send(FT.at[n, pl.ds(pl.multiple_of(32 * s, 32), 32)], TA.at[n, d, t], d, s)
+        TA[n, d, t] = FT[n, pl.ds(pl.multiple_of(32 * t, 32), 32), :]
+
+    for cp in rs_cp:
+        cp.wait_recv()
+    w_own = WC[pl.ds(pl.multiple_of(128 * c, 128), 128), :]
+    lane = lax.broadcasted_iota(jnp.int32, (4, 128), 1)
+    gain_sum = jnp.zeros((128, 1), f32)
+    grad_reduce = jnp.zeros((128, 256), f32)
+    for n, p in enumerate((z, partner, far_mid, far_end)):
+        if n >= 2:
+            grad_gather.forward(far_end, n - 2)
+        if n == 3:
+            gp = pooled_sum.result(GP[...])
+            gp_high, gp_low = split(gp)
+            FT[0] = mm(act_live, gp_high, 0, 0).astype(bf16)
+            turn_cp = list(turn(0))
+            for m in range(4):
+                cells = slice(288 * m, 288 * (m + 1))
+                SP[:, 1152 * m : 1152 * (m + 1)] = mm(gp_high[cells], POOL[...], 0, 0) + mm(gp_low[cells], POOL[...], 0, 0)
+            for cp in cgd_cp:
+                cp.wait_recv()
+            total = CGD[0].astype(f32)
+            for m in range(1, 4):
+                total += CGD[m].astype(f32)
+            CGT[...] = total.astype(bf16)
+            cgz_cp = [send(CGT.at[(z + k) % 4], CGZ.at[z], d, zpeer(k)) for k in range(1, 4)]
+            CGZ[z] = CGT[z]
+        grad_gather.ready(n)
+        cols = pl.ds(pl.multiple_of(1152 * p, 128), 1152)
+        even, odd = RS[2 * p], RS[2 * p + 1]
+        stats = jnp.concatenate([even[:, 0:512], jnp.where(lane < 64, even[:, 512:640], odd[:, 0:128]), odd[:, 128:640]], axis=1)
+        g = GA[pl.ds(2 * p, 2)].reshape(1152, 256)
+        xhat = (PLC[:, cols] - stats[0:1]) * stats[1:2]
+        grad_reduce += mm((xhat * go).astype(bf16), g, 1, 0)
+        if n == 3:
+            FT[1] = jnp.transpose(grad_reduce).astype(bf16)
+            turn_cp += list(turn(1))
+        gn = mm(w_own, g, 1, 1)
+        gain_sum += jnp.sum(gn * xhat, axis=1, keepdims=True)
+        GF[:, cols] = stats[1:2] * (gn * go - stats[2:3] - xhat * stats[3:4])
+    for cp in turn_cp[0:7]:
+        cp.wait_recv()
+    ta_cp = [send(TA.at[0, d], TA.at[0, d], dpeer(k), t) for k in range(1, 4)]
+    place_sum = jnp.zeros((128, 1152), f32)
+    for p in range(4):
+        cols = slice(1152 * p, 1152 * (p + 1))
+        out = GF[:, cols] + SP[:, cols]
+        GF[:, cols] = out
+        store(GF.at[:, cols], gfeat_o.at[:, cols])
+        place_sum += out
+    odd = pltpu.roll(place_sum, 576, 1)
+    lane = lax.broadcasted_iota(jnp.int32, (128, 640), 1)
+    place = jnp.where(lane < 576, place_sum[:, 0:640] + odd[:, 0:640], jnp.broadcast_to(gain_sum, (128, 640))).astype(bf16)
+    for q in range(4):
+        PM[q] = place[32 * q : 32 * (q + 1)]
+    pm_cp = [send(PM.at[dpeer(k)], PR.at[d], dpeer(k), t) for k in range(1, 4)]
+    PR[d] = PM[d]
+
+    for cp in turn_cp[7:14]:
+        cp.wait_recv()
+    ta_cp += [send(TA.at[1, d], TA.at[1, d], dpeer(k), t) for k in range(1, 4)]
+    for cp in pm_cp:
+        cp.wait_recv()
+    total = PR[0].astype(f32)
     for n in range(1, 4):
-        total += CGD[n].astype(f32)
-    CGT[...] = total.astype(bf16)
-    cgz_cp = [send(CGT.at[(z + k) % 4], CGZ.at[z], d, zpeer(k)) for k in range(1, 4)]
-    CGZ[z] = CGT[z]
-    gp = pooled_sum.result(GP[...])
-    gp_high, gp_low = split(gp)
-    FT[0] = mm(act_live, gp_high, 0, 0).astype(bf16)
+        total += PR[n].astype(f32)
+    PF[d] = total.astype(bf16)
+    pf_cp = [send(PF.at[d], PF.at[d], dpeer(k), t) for k in range(1, 4)]
     for cp in cgz_cp:
         cp.wait_recv()
     total = CGZ[0].astype(f32)
-    for n in range(1, 4):
-        total += CGZ[n].astype(f32)
+    for m in range(1, 4):
+        total += CGZ[m].astype(f32)
     CGF[d] = total.astype(bf16)
     cgf_cp = [send(CGF.at[d], CGF.at[d], dpeer(k), t) for k in range(1, 4)]
-    for cp in rs_cp:
-        cp.wait_recv()
-    grad_gather.finish()
-    w_own = WC[pl.ds(pl.multiple_of(128 * c, 128), 128), :]
-    lane = lax.broadcasted_iota(jnp.int32, (4, 128), 1)
-    place_sum = jnp.zeros((128, 1152), f32)
-    gain_sum = jnp.zeros((128, 1), f32)
-    grad_reduce = jnp.zeros((128, 256), f32)
-    for p in range(4):
-        cols = slice(1152 * p, 1152 * (p + 1))
-        even, odd = RS[2 * p], RS[2 * p + 1]
-        stats = jnp.concatenate([even[:, 0:512], jnp.where(lane < 64, even[:, 512:640], odd[:, 0:128]), odd[:, 128:640]], axis=1)
-        g = GA[2 * p : 2 * p + 2].reshape(1152, 256)
-        gn = mm(w_own, g, 1, 1)
-        xhat = (PLC[:, cols] - stats[0:1]) * stats[1:2]
-        gain_sum += jnp.sum(gn * xhat, axis=1, keepdims=True)
-        grad_reduce += mm((xhat * go).astype(bf16), g, 1, 0)
-        spread = mm(gp_high[288 * p : 288 * (p + 1)], POOL[...], 0, 0) + mm(gp_low[288 * p : 288 * (p + 1)], POOL[...], 0, 0)
-        out = spread + stats[1:2] * (gn * go - stats[2:3] - xhat * stats[3:4])
-        gfeat_o[:, cols] = out
-        place_sum += out
-    FT[1] = jnp.transpose(grad_reduce).astype(bf16)
-    ft_cp = []
-    for k in range(1, 8):
-        s = (t + k) % 8
-        ft_cp.append(send(FT.at[:, pl.ds(pl.multiple_of(32 * s, 32), 32)], TA.at[d, t], d, s))
-    TA[d, t] = FT[:, pl.ds(pl.multiple_of(32 * t, 32), 32), :]
-    odd = pltpu.roll(place_sum, 576, 1)
-    lane = lax.broadcasted_iota(jnp.int32, (128, 640), 1)
-    PM[d] = jnp.where(lane < 576, place_sum[:, 0:640] + odd[:, 0:640], jnp.broadcast_to(gain_sum, (128, 640))).astype(bf16)
-    pm_cp = [send(PM.at[d], PM.at[d], dpeer(k), t) for k in range(1, 4)]
-    for cp in ft_cp:
-        cp.wait_recv()
-    ta_cp = [send(TA.at[d], TA.at[d], dpeer(k), t) for k in range(1, 4)]
-
     for cp in grf_cp:
         cp.wait_recv()
     for q in range(4):
-        gread_o[128 * q : 128 * (q + 1), :] = GRF[q].astype(f32)
+        store(GRF.at[q], gread_o.at[pl.ds(128 * q, 128)])
     for cp in cgf_cp:
         cp.wait_recv()
     for q in range(4):
-        gconv_o[:, 640 * q : 640 * (q + 1)] = CGF[q].astype(f32)
-    for cp in pm_cp:
-        cp.wait_recv()
-    total = PM[0].astype(f32)
-    for n in range(1, 4):
-        total += PM[n].astype(f32)
-    gpos_o[...] = jnp.transpose(total)
+        gconv_o[:, 640 * q : 640 * (q + 1)] = CGF[q]
     for cp in ta_cp:
         cp.wait_recv()
-    for s in range(8):
-        total = TA[0, s].astype(f32)
-        for n in range(1, 4):
-            total += TA[n, s].astype(f32)
-        gexp_o[:, 128 * s : 128 * (s + 1)] = total[0]
-        gred_o[:, 128 * s : 128 * (s + 1)] = total[1]
+    for n, out in enumerate((gexp_o, gred_o)):
+        for s in range(8):
+            total = TA[n, 0, s].astype(f32)
+            for m in range(1, 4):
+                total += TA[n, m, s].astype(f32)
+            out[:, 128 * s : 128 * (s + 1)] = total
+    for cp in pf_cp:
+        cp.wait_recv()
+    gpos_o[...] = jnp.transpose(PF[...].reshape(128, 640).astype(f32))
+    for cp in result_cp:
+        cp.wait()
     for cp in pending:
         cp.wait_send()
     placed_gather.drain()
@@ -547,46 +613,110 @@
 
 
 SCRATCH = (
-    ("WBLK", (32, 1024), bf16), ("WT", (256, 256), bf16), ("WC", (256, 256), bf16), ("CB", (32, 3584), bf16),
+    ("readout_weight", (512, 1024), bf16), ("cotangent", (512, 1152), bf16), ("RO", (512, 1152), bf16), ("GF", (128, 4608), f32), ("SP", (128, 4608), f32), ("WT", (256, 256), bf16), ("WC", (256, 256), bf16), ("CB", (32, 3584), bf16),
     ("WQ", (4, 32, 896), bf16), ("WB", (2, 4, 4, 32, 896), bf16), ("WF", (256, 3584), bf16), ("MT", (512, 256), bf16),
     ("POOL", (288, 1152), bf16), ("PLC", (128, 4608), f32), ("XW", (2, 4, 128, 640), bf16), ("XK", (4, 256, 640), bf16),
     ("ST", (8, 4, 640), f32), ("SR", (8, 4, 640), f32), ("QF", (640, 256), f32), ("QS", (3, 576, 256), bf16),
     ("QO", (576, 256), f32), ("QR", (4, 576, 256), bf16), ("RED", (24, 32, 256), f32), ("HB", (832, 768), bf16),
     ("GB", (832, 256), bf16), ("XM", (768, 256), f32), ("ZM", (768, 256), f32), ("RM", (768, 128), f32),
     ("XI", (768, 256), f32), ("ZI", (768, 256), f32), ("RI", (768, 128), f32), ("ACT", (8, 144, 256), bf16), ("ACL", (8, 144, 256), bf16),
-    ("PP", (8, 1152, 128), bf16), ("POOLED", (1152, 1024), bf16), ("BEF", (512, 1152), f32), ("GBT", (512, 1152), bf16),
+    ("PP", (8, 1152, 128), bf16), ("POOLED", (1152, 1024), bf16), ("BEF", (512, 1152), f32), ("GBT", (512, 1152), bf16), ("GBR", (1152, 512), bf16),
     ("TE", (2, 4, 1152, 128), bf16), ("TR", (4, 1152, 128), bf16), ("ES", (3, 1152, 128), bf16), ("ER", (4, 1152, 128), bf16),
     ("GP", (1152, 128), f32), ("AT", (2, 4, 144, 256), bf16), ("AR", (4, 144, 256), bf16), ("AS", (3, 144, 256), bf16),
-    ("AZ", (3, 144, 256), bf16), ("GW", (8, 128), f32), ("GA", (8, 576, 256), bf16), ("RS", (8, 4, 640), f32),
-    ("FT", (2, 256, 128), bf16), ("TA", (4, 8, 2, 32, 128), bf16), ("PM", (4, 128, 640), bf16),
+    ("AZ", (3, 144, 256), bf16), ("RSC", (640, 128), f32), ("GA", (8, 576, 256), bf16), ("RS", (8, 4, 640), f32),
+    ("FT", (2, 256, 128), bf16), ("TA", (2, 4, 8, 32, 128), bf16), ("PM", (4, 32, 640), bf16),
+    ("PR", (4, 32, 640), bf16), ("PF", (4, 32, 640), bf16),
     ("CG", (2, 4, 32, 2560), bf16), ("CGR", (4, 32, 2560), bf16), ("CGS", (4, 32, 2560), bf16), ("CGD", (4, 4, 32, 640), bf16),
     ("CGT", (4, 32, 640), bf16), ("CGZ", (4, 32, 640), bf16), ("CGF", (4, 32, 640), bf16), ("GR", (4, 128, 1024), bf16), ("GRR", (4, 128, 1024), bf16),
     ("GRF", (4, 128, 1024), bf16),
 )
 
 
+def finish(
+    readout, gfeat, gpos, gexp, gred, gconv, gread, readout_o, gfeat_o, gpos_o, ggo_o, gred_o, ggm_o, gconv_o, ggi_o, gexp_o, gread_o,
+    RO, GF, GB, GC, GR, GP, GQ, GE, GD, sem,
+):
+    copies = []
+
+    def copy(src, dst):
+        cp = pltpu.make_async_copy(src, dst, sem.at[len(copies)])
+        copies.append(cp)
+        cp.start()
+        return cp
+
+    loads = [copy(gread.at[pl.ds(256 * p, 256)], GB.at[pl.ds(256 * p, 256)]) for p in range(2)]
+    loads += [copy(gfeat.at[pl.ds(32 * p, 32)], GF.at[pl.ds(32 * p, 32)]) for p in range(4)]
+    loads += [copy(readout, RO), copy(gconv, GC), copy(gpos, GP), copy(gexp, GE), copy(gred, GD)]
+    stores = []
+    for p in range(2):
+        rows = pl.ds(256 * p, 256)
+        loads[p].wait()
+        GR[rows, :] = GB[rows, :].astype(f32)
+        stores.append(copy(GR.at[rows], gread_o.at[rows]))
+    for p in range(4):
+        rows = pl.ds(32 * p, 32)
+        loads[2 + p].wait()
+        stores.append(copy(GF.at[rows], gfeat_o.at[rows]))
+    loads[6].wait()
+    stores.append(copy(RO, readout_o))
+    loads[7].wait()
+    for n in range(9):
+        GQ[n] = GC[:, 256 * n : 256 * (n + 1)].astype(f32)
+    stores.append(copy(GQ, gconv_o))
+    first = (lax.broadcasted_iota(jnp.int32, (8, 128), 1) == 0).astype(f32).astype(bf16)
+    ggi_o[...] = mm(first, GC[:, 2304:2432], 1, 1)[0:1]
+    ggm_o[...] = mm(first, GC[:, 2432:2560], 1, 1)[0:1]
+    loads[8].wait()
+    stores.append(copy(GP.at[pl.ds(0, 576)], gpos_o))
+    ggo_o[...] = GP[576:577, :]
+    loads[9].wait()
+    stores.append(copy(GE, gexp_o))
+    loads[10].wait()
+    stores.append(copy(GD, gred_o))
+    for cp in stores:
+        cp.wait()
+
+
 def local_by_image(features, slot_live, position, gain_outer, reduce_weight, gain_middle, conv_weight, gain_inner, expand_weight, readout_weight, cotangent):
     vmem = pl.BlockSpec(memory_space=pltpu.VMEM)
     smem = pl.BlockSpec(memory_space=pltpu.SMEM)
-    readout, gfeat, gpos, gexp, gred, gconv, gread = pl.pallas_call(
+    hbm = pl.BlockSpec(memory_space=pl.ANY)
+
+    def shapes(*pairs):
+        return tuple(jax.ShapeDtypeStruct(shape, dtype) for shape, dtype in pairs)
+
+    parts = pl.pallas_call(
         kernel,
-        out_shape=(
-            jax.ShapeDtypeStruct((512, 1152), bf16), jax.ShapeDtypeStruct((128, 4608), f32), jax.ShapeDtypeStruct((640, 128), f32),
-            jax.ShapeDtypeStruct((32, 1024), f32), jax.ShapeDtypeStruct((32, 1024), f32), jax.ShapeDtypeStruct((32, 2560), f32),
-            jax.ShapeDtypeStruct((512, 1024), f32),
+        out_shape=shapes(
+            ((512, 1152), bf16), ((128, 4608), f32), ((640, 128), f32), ((32, 1024), f32), ((32, 1024), f32), ((32, 2560), bf16), ((512, 1024), bf16)
         ),
-        in_specs=[vmem, smem] + [vmem] * 9,
-        out_specs=[vmem] * 7,
+        in_specs=[vmem, smem] + [vmem] * 7 + [hbm] * 2,
+        out_specs=[hbm, hbm, vmem, vmem, vmem, vmem, hbm],
         scratch_shapes=[pltpu.VMEM(shape, dtype) for _, shape, dtype in SCRATCH]
-        + [pltpu.SemaphoreType.DMA((COPIES,)), pltpu.SemaphoreType.DMA((COPIES,))],
-        compiler_params=pltpu.CompilerParams(collective_id=0, has_side_effects=True, vmem_limit_bytes=63 * 2**20),
+        + [pltpu.SemaphoreType.DMA((COPIES,)), pltpu.SemaphoreType.DMA((COPIES,)), pltpu.SemaphoreType.DMA((16,))],
+        compiler_params=pltpu.CompilerParams(collective_id=0, has_side_effects=True, vmem_limit_bytes=60 * 2**20),
     )(
-        features, slot_live, position.reshape(576, 128), gain_outer.reshape(1, 128), reduce_weight, gain_middle.reshape(1, 32),
-        conv_weight.reshape(2304, 32), gain_inner.reshape(1, 32), expand_weight, readout_weight, cotangent,
-    )
+        features, slot_live, position.reshape(576, 128), gain_outer.reshape(1, 128), reduce_weight.T, gain_middle.reshape(1, 32),
+        conv_weight.transpose(0, 1, 3, 2).reshape(9, 32, 256), gain_inner.reshape(1, 32), expand_weight, readout_weight, cotangent,
+    )
+    readout, gfeat, gpos, ggo, gred, ggm, gconv, ggi, gexp, gread = pl.pallas_call(
+        finish,
+        out_shape=shapes(
+            ((512, 1152), bf16), ((128, 4608), f32), ((576, 128), f32), ((1, 128), f32), ((32, 1024), f32), ((1, 32), f32),
+            ((9, 32, 256), f32), ((1, 32), f32), ((32, 1024), f32), ((512, 1024), f32),
+        ),
+        in_specs=[hbm] * 7,
+        out_specs=[hbm, hbm, hbm, vmem, hbm, vmem, hbm, vmem, hbm, hbm],
+        scratch_shapes=[
+            pltpu.VMEM((512, 1152), bf16), pltpu.VMEM((128, 4608), f32), pltpu.VMEM((512, 1024), bf16), pltpu.VMEM((32, 2560), bf16),
+            pltpu.VMEM((512, 1024), f32), pltpu.VMEM((640, 128), f32), pltpu.VMEM((9, 32, 256), f32), pltpu.VMEM((32, 1024), f32),
+            pltpu.VMEM((32, 1024), f32), pltpu.SemaphoreType.DMA((24,)),
+        ],
+        compiler_params=pltpu.CompilerParams(vmem_limit_bytes=60 * 2**20),
+    )(*parts)
     return (
-        readout, gfeat, gpos[0:576].reshape(24, 24, 128), gpos[576], gred.T, gconv[:, 2432],
-        gconv[:, 0:2304].T.reshape(3, 3, 256, 32), gconv[:, 2304], gexp, gread,
+        readout, gfeat, gpos.reshape(24, 24, 128), ggo.reshape(128), gred.T, ggm.reshape(32),
+        gconv.reshape(3, 3, 32, 256).transpose(0, 1, 3, 2), ggi.reshape(32), gexp, gread,
     )
 
 

time: 160 us -> 143 us (0.89)
  local copies, waits for them, and re-layouts: 16.4 us -> 0 us
    unnamed x16 -> x0, local copies, waits for them, and re-layouts: 10.8 us -> none
    slice x2 -> x0, local copies, waits for them, and re-layouts: 3.06 us -> none  [the longest x1 1.69 us: local_by_image(): gpos[0:576].reshape(24, 24, 128)]
    pallas_call x1 -> x2, Pallas kernels: 142 us -> 142 us  [the longest x1 137 us: local_by_image(): pl.pallas_call(kernel, out_shape=shapes(((512, 1152), bf16), ((128, 4608)...]
where the time goes in v4:
time: 143 us
  Pallas kernels  142 us (99%)
    pallas_call x1, Pallas kernels, local_by_image(): pl.pallas_call(kernel, out_shape=shapes(((512, 1152), bf16), ((128, 4608)...  137 us
    pallas_call x1, Pallas kernels, local_by_image(): pl.pallas_call(finish, out_shape=shapes(((512, 1152), bf16), ((128, 4608)...  5.04 us

profile of v4, /device:TPU:0, one launch (start us, length us, event | category | flops | bytes accessed | tf_op | source)
XLA Modules:
  0.0 143.2 jit_solution(15045053645673325649)
XLA Ops:
  0.6 137.3 %shard_map.186 = (bf16[512,1152]{1,0:T(8,128)(2,1)}, f32[128,4608]{1,0:T(8,128)}, f32[640,128]{1,0:T(8,128)}, f32[32,1024]{1,0:T(8,128)}, f32[32,1024]{1,0:T(8,1...) custom-call(bf16[128,4608]{1,0:T(8,128)(2,1)} %features.1, s32[8]{0:T(128)} %slot_live.1, f32[576,128]{1,0:T(8,128)} %bitcast.16, ...), custom_call_target="tpu_custom_call" | custom-call | tf_op jit(solution)/shard_map/pallas_call | solution.py:688
  138.0 5.0 %shard_map.187 = (bf16[512,1152]{1,0:T(8,128)(2,1)}, f32[128,4608]{1,0:T(8,128)}, f32[576,128]{1,0:T(8,128)}, f32[1,128]{1,0:T(1,128)}, f32[32,1024]{1,0:T(8,128...) custom-call(bf16[512,1152]{1,0:T(8,128)(2,1)} %get-tuple-element.27., ...), custom_call_target="tpu_custom_call" | custom-call | tf_op jit(solution)/shard_map/pallas_call | solution.py:702

commit v5 on v4

--- a/solution.py
+++ b/solution.py
@@ -53,9 +53,9 @@
 
 
 def kernel(
-    features, slot_live, position, gain_outer, reduce_weight, gain_middle, conv_weight, gain_inner, expand_weight, readout_h, cotangent_h,
+    features_h, slot_live, position_h, gain_outer, reduce_weight, gain_middle, conv_h, gain_inner, expand_h, readout_h, cotangent_h,
     readout_o, gfeat_o, gpos_o, gexp_o, gred_o, gconv_o, gread_o,
-    readout_weight, cotangent, RO, GF, SP, WT, WC, CB, WQ, WB, WF, MT, POOL, PLC, XW, XK, ST, SR, QF, QS, QO, QR, RED, HB, GB,
+    features, position, conv_weight, expand_weight, readout_weight, cotangent, RO, GF, SP, WT, WC, CB, WQ, WB, WF, MT, POOL, PLC, XW, XK, ST, SR, QF, QS, QO, QR, RED, HB, GB,
     XM, ZM, RM, XI, ZI, RI, ACT, ACL, PP, POOLED, BEF, GBT, GBR, TE, TR, ES, ER, GP, AT, AR, AS, AZ,
     RSC, GA, RS, FT, TA, PM, PR, PF, CG, CGR, CGS, CGD, CGT, CGZ, CGF, GR, GRR, GRF, ssem, rsem, lsem,
 ):
@@ -125,20 +125,20 @@
                 self.arrived(block, h)
                 cp.start()
 
+        def pass_on(self, n):
+            for h in range(self.parts):
+                if n == 3:
+                    self.arrived(blocks[n], h)
+                else:
+
+                    @pl.when(is_mid == 0)
+                    def _(h=h):
+                        self.arrived(blocks[n], h)
+
+            slot = self.buf.at[2 * blocks[n] + c]
+            self.siblings.append(send(slot, slot, d, sib))
+
         def ready(self, n):
-            if n > 0:
-                block = (partner, far_mid, far_end)[n - 1]
-                for h in range(self.parts):
-                    if n == 1:
-                        self.arrived(block, h)
-                    else:
-
-                        @pl.when(is_mid == 0)
-                        def _(h=h):
-                            self.arrived(block, h)
-
-                slot = self.buf.at[2 * block + c]
-                self.siblings.append(send(slot, slot, d, sib))
             self.siblings[n].wait_recv()
 
         def drain(self):
@@ -152,6 +152,8 @@
         far_mid + is_mid * (far_end - far_mid),
         near_mid + is_mid * (far_mid - near_mid),
     )
+
+    blocks = (z, partner + is_mid * (far_mid - partner), far_mid + is_mid * (far_end - far_mid), far_end + is_mid * (partner - far_end))
 
     class Summed:
         def __init__(self, out, arrive):
@@ -195,16 +197,15 @@
     def dpeer(k):
         return (d + k) % 4
 
-    operand_cp = [
-        pltpu.make_async_copy(readout_h, readout_weight, lsem.at[0]),
-        pltpu.make_async_copy(cotangent_h, cotangent, lsem.at[1]),
-    ]
-    for cp in operand_cp:
+    def load(n, src, dst):
+        cp = pltpu.make_async_copy(src, dst, lsem.at[n])
         cp.start()
+        return cp
+
     result_cp = []
 
     def store(src, dst):
-        cp = pltpu.make_async_copy(src, dst, lsem.at[2 + len(result_cp)])
+        cp = pltpu.make_async_copy(src, dst, lsem.at[9 + len(result_cp)])
         cp.start()
         result_cp.append(cp)
 
@@ -214,21 +215,13 @@
     for k in range(1, 4):
         pl.semaphore_signal(barrier, 1, device_id=(dpeer(k), t), device_id_type=MESH)
 
-    for n in range(9):
-        CB[:, 256 * n : 256 * (n + 1)] = conv_weight[n]
-    CB[:, 2304:3328] = expand_weight[...]
-    eighth = jnp.full((8, 128), 0.125, f32)
-    lane = lax.broadcasted_iota(jnp.int32, (32, 128), 1)
-    packed = jnp.zeros((32, 128), f32)
-    for n, gain in enumerate((gain_middle, gain_inner)):
-        column = mm(jnp.broadcast_to(gain[...], (8, 32)), eighth, 0, 0, HIGHEST)
-        high, rest = split(column)
-        rest = column - high.astype(f32)
-        mid, low = split(rest)
-        for m, part in enumerate((high, mid, low)):
-            packed = jnp.where(lane == 3 * n + m, part.astype(f32), packed)
-    CB[:, 3328:3456] = packed.astype(bf16)
-    CB[:, 3456:3584] = jnp.zeros((32, 128), bf16)
+    position_cp = load(0, position_h, position)
+    feature_cp = []
+    for n, p in enumerate((*order, z)):
+        cols = pl.ds(pl.multiple_of(1152 * p, 128), 1152)
+        feature_cp.append(load(1 + n, features_h.at[:, cols], features.at[:, cols]))
+    weight_cp = [load(5, conv_h, conv_weight), load(6, expand_h, expand_weight)]
+    operand_cp = [load(7, readout_h, readout_weight), load(8, cotangent_h, cotangent)]
     POOL[...] = pool_pair()
     pl.semaphore_wait(barrier, 10)
 
@@ -237,19 +230,16 @@
         s = (t + k) % 8
         w_cp.append(send(reduce_weight.at[:, pl.ds(pl.multiple_of(256 * (s // 2), 256), 256)], WT.at[pl.ds(pl.multiple_of(32 * t, 32), 32)], d, s))
     WT[pl.ds(pl.multiple_of(32 * t, 32), 32), :] = reduce_weight[:, pl.ds(pl.multiple_of(256 * z, 256), 256)]
-    quarter = CB.at[:, pl.ds(pl.multiple_of(896 * d, 128), 896)]
-    wq_cp = [send(quarter, WQ.at[z], d, zpeer(k)) for k in range(1, 4)]
-    WQ[z] = quarter[...]
-    WB[c, d, z] = quarter[...]
-    wb_cp = [send(WQ.at[z], WB.at[c, d, z], dpeer(k), t) for k in range(1, 4)]
-
+    position_cp.wait()
     go_rows = jnp.broadcast_to(gain_outer[...], (8, 128))
+    eighth = jnp.full((8, 128), 0.125, f32)
     go = mm(go_rows, eighth, 0, 0, HIGHEST)[:, 0:1]
     pos = position[...]
     pos_pair = mm(eye(128, f32), jnp.concatenate([pos, pos], axis=0), 1, 1, HIGHEST)
     x_cp = []
-    for p in (*order, z):
+    for n, p in enumerate((*order, z)):
         cols = pl.ds(pl.multiple_of(1152 * p, 128), 1152)
+        feature_cp[n].wait()
         x = features[:, cols].astype(f32) + pos_pair
         PLC[:, cols] = x
         m = jnp.mean(x, axis=0, keepdims=True)
@@ -263,6 +253,33 @@
         x_cp.append(send(XW.at[1 - c, p], XK.at[p, pl.ds(pl.multiple_of(128 * c, 128), 128)], d, sib))
         XK[p, pl.ds(pl.multiple_of(128 * c, 128), 128), :] = XW[c, p]
 
+    for p in range(4):
+        high, low = split(PLC[:, 1152 * p : 1152 * (p + 1)])
+        PP[t, 288 * p : 288 * (p + 1), :] = (mm(POOL[...], high, 1, 1) + mm(POOL[...], low, 1, 1)).astype(bf16)
+    placed_gather = Gather(PP, 1)
+    placed_gather.start(far_mid)
+    for cp in weight_cp:
+        cp.wait()
+    for n in range(9):
+        CB[:, 256 * n : 256 * (n + 1)] = conv_weight[n]
+    CB[:, 2304:3328] = expand_weight[...]
+    lane = lax.broadcasted_iota(jnp.int32, (32, 128), 1)
+    packed = jnp.zeros((32, 128), f32)
+    for n, gain in enumerate((gain_middle, gain_inner)):
+        column = mm(jnp.broadcast_to(gain[...], (8, 32)), eighth, 0, 0, HIGHEST)
+        high, rest = split(column)
+        rest = column - high.astype(f32)
+        mid, low = split(rest)
+        for m, part in enumerate((high, mid, low)):
+            packed = jnp.where(lane == 3 * n + m, part.astype(f32), packed)
+    CB[:, 3328:3456] = packed.astype(bf16)
+    CB[:, 3456:3584] = jnp.zeros((32, 128), bf16)
+    quarter = CB.at[:, pl.ds(pl.multiple_of(896 * d, 128), 896)]
+    wq_cp = [send(quarter, WQ.at[z], d, zpeer(k)) for k in range(1, 4)]
+    WQ[z] = quarter[...]
+    WB[c, d, z] = quarter[...]
+    wb_cp = [send(WQ.at[z], WB.at[c, d, z], dpeer(k), t) for k in range(1, 4)]
+
     for cp in w_cp:
         cp.wait_recv()
     WC[...] = mm(eye(256), WT[...], 1, 1).astype(bf16)
@@ -270,8 +287,6 @@
     colsum = mm(go_rows, mine, 1, 0, HIGHEST)[0:1]
     for n in range(8):
         ST[n, 2:3, 0:256] = colsum
-    st_cp = [send(ST.at[(t + k) % 8], SR.at[t], d, (t + k) % 8) for k in range(1, 8)]
-    SR[t] = ST[t]
     reduced_sum = Summed(QS, QR)
     for n, p in enumerate((*order, z)):
         x_cp[n].wait_recv()
@@ -282,11 +297,9 @@
         else:
             QS[n] = part.astype(bf16)
             reduced_sum.start(n)
-    for p in range(4):
-        high, low = split(PLC[:, 1152 * p : 1152 * (p + 1)])
-        PP[t, 288 * p : 288 * (p + 1), :] = (mm(POOL[...], high, 1, 1) + mm(POOL[...], low, 1, 1)).astype(bf16)
-    placed_gather = Gather(PP, 1)
-    placed_gather.start(far_mid)
+        if n == 0:
+            st_cp = [send(ST.at[(t + k) % 8], SR.at[t], d, (t + k) % 8) for k in range(1, 8)]
+            SR[t] = ST[t]
     placed_gather.start(partner)
     placed_gather.own()
 
@@ -299,14 +312,25 @@
     reduced_sum.add(0)
     placed_gather.forward(far_mid, 0)
     reduced_sum.add(1)
-    for cp in wb_cp:
-        cp.wait_recv()
-    ws_cp = send(WB.at[c], WB.at[c], d, sib)
-    ws_cp.wait_recv()
-    for cc in range(2):
-        for zz in range(4):
-            for dd in range(4):
-                WF[32 * (2 * zz + cc) : 32 * (2 * zz + cc + 1), 896 * dd : 896 * (dd + 1)] = WB[cc, dd, zz]
+    ws_cp = [send(WB.at[c, d], WB.at[c, d], d, sib)]
+    for k in range(1, 4):
+        for n in range(4):
+            wb_cp[3 * n + k - 1].wait_recv()
+        quarter = (d + 4 - k) % 4
+        ws_cp.append(send(WB.at[c, quarter], WB.at[c, quarter], d, sib))
+    for cp in ws_cp:
+        cp.wait_recv()
+
+    def spread_out(lo, hi):
+        for cc in range(2):
+            for zz in range(4):
+                rows = slice(32 * (2 * zz + cc), 32 * (2 * zz + cc + 1))
+                for dd in range(lo // 896, (hi + 895) // 896):
+                    x, y = max(lo, 896 * dd), min(hi, 896 * (dd + 1))
+                    WF[rows, x:y] = WB[cc, dd, zz, :, x - 896 * dd : y - 896 * dd]
+
+    spread_out(0, 2304)
+    spread_out(3328, 3456)
     lane = lax.broadcasted_iota(jnp.int32, (8, 128), 1)
     row = lax.broadcasted_iota(jnp.int32, (8, 128), 0)
     pick = jnp.where((lane >= 3 * row) & (lane < 3 * row + 3) & (row < 2), 1.0, 0.0).astype(bf16)
@@ -355,13 +379,18 @@
     placed_gather.forward(far_end, 0)
     for cp in operand_cp:
         cp.wait()
+    spread_out(2304, 3328)
     MT[...] = mm(readout_weight[...], WF[:, 2304:3328], 1, 1).astype(bf16)
-    for n, q in enumerate((z, partner, far_mid, far_end)):
-        if n == 2:
+    for n, q in enumerate(blocks):
+        if n == 0:
+            placed_gather.pass_on(1)
+            placed_gather.pass_on(2)
+        if n == 3:
             for k in range(1, 4):
                 a_cp[k - 1].wait_recv()
                 slot = 2 * ((z + 4 - k) % 4) + c
                 as_cp.append(send(ACT.at[slot], ACT.at[slot], d, sib))
+            placed_gather.pass_on(3)
         placed_gather.ready(n)
         both = jnp.concatenate([PP[2 * q], PP[2 * q + 1]], axis=1)
         part = mm(readout_weight[:, pl.ds(pl.multiple_of(256 * q, 256), 256)], both, 1, 1)
@@ -401,7 +430,8 @@
     def pooled_block(n):
         te_cp[n].wait_recv()
         ES[n] = (TE[c, order[n]].astype(f32) + TR[order[n]].astype(f32)).astype(bf16)
-        pooled_sum.start(n)
+        if n < 2:
+            pooled_sum.start(n)
 
     for n, q in enumerate((*order, z)):
         block = mm(GBR[...], readout_weight[:, pl.ds(pl.multiple_of(256 * q, 256), 256)], 1, 0).astype(bf16)
@@ -456,7 +486,7 @@
     dyx_middle = dy * xm
     gr = norm_rows_back(dy * gm, xm, RM[:, 0:1]).reshape(24, 32, 256)[:, 0:24, :].reshape(576, 256).astype(bf16)
     GA[t] = gr
-    grad_gather = Gather(GA, 2)
+    grad_gather = Gather(GA, 4)
     grad_gather.start(far_mid)
     wg = jnp.sum(sums, axis=0, keepdims=True)
     grad_rounded = gr.astype(f32)
@@ -472,8 +502,17 @@
     RS[t, 2:4, :] = row_sums[0:2]
     rs_cp = [send(RS.at[t], RS.at[t], d, (t + k) % 8) for k in range(1, 8)]
     grad_gather.start(partner)
+    pooled_sum.start(2)
     grad_gather.own()
     pooled_sum.add(1)
+
+    for cp in gr_cp:
+        cp.wait_recv()
+    total = GRR[0].astype(f32)
+    for n in range(1, 4):
+        total += GRR[n].astype(f32)
+    GRF[d] = total.astype(bf16)
+    grf_cp = [send(GRF.at[d], GRF.at[d], dpeer(k), t) for k in range(1, 4)]
 
     def put(lo, value):
         value = value.astype(bf16)
@@ -488,13 +527,6 @@
         put(lo, mm(high, ones, 0, 0) + mm(low, ones, 0, 0))
     cg_cp = send(CG.at[1 - c], CGR, d, sib)
 
-    for cp in gr_cp:
-        cp.wait_recv()
-    total = GRR[0].astype(f32)
-    for n in range(1, 4):
-        total += GRR[n].astype(f32)
-    GRF[d] = total.astype(bf16)
-
     cg_cp.wait_recv()
     CGS[...] = (CG[c].astype(f32) + CGR[...].astype(f32)).astype(bf16)
     cgd_cp = []
@@ -502,9 +534,8 @@
         dd = dpeer(k)
         cgd_cp.append(send(CGS.at[:, :, pl.ds(pl.multiple_of(640 * dd, 128), 640)], CGD.at[d], dd, t))
     CGD[d] = CGS[:, :, pl.ds(pl.multiple_of(640 * d, 128), 640)]
-    grf_cp = [send(GRF.at[d], GRF.at[d], dpeer(k), t) for k in range(1, 4)]
-
-    for h in range(2):
+
+    for h in range(4):
         grad_gather.forward(far_mid, h)
     def turn(n):
         for k in range(1, 8):
@@ -518,10 +549,13 @@
     lane = lax.broadcasted_iota(jnp.int32, (4, 128), 1)
     gain_sum = jnp.zeros((128, 1), f32)
     grad_reduce = jnp.zeros((128, 256), f32)
-    for n, p in enumerate((z, partner, far_mid, far_end)):
-        if n >= 2:
-            grad_gather.forward(far_end, n - 2)
-        if n == 3:
+    for n, p in enumerate(blocks):
+        if n == 0:
+            grad_gather.pass_on(1)
+        if n == 1:
+            for h in range(4):
+                grad_gather.forward(far_end, h)
+            grad_gather.pass_on(2)
             gp = pooled_sum.result(GP[...])
             gp_high, gp_low = split(gp)
             FT[0] = mm(act_live, gp_high, 0, 0).astype(bf16)
@@ -537,6 +571,18 @@
             CGT[...] = total.astype(bf16)
             cgz_cp = [send(CGT.at[(z + k) % 4], CGZ.at[z], d, zpeer(k)) for k in range(1, 4)]
             CGZ[z] = CGT[z]
+        if n == 3:
+            for cp in turn_cp[0:7]:
+                cp.wait_recv()
+            ta_cp = [send(TA.at[0, d], TA.at[0, d], dpeer(k), t) for k in range(1, 4)]
+            for cp in cgz_cp:
+                cp.wait_recv()
+            total = CGZ[0].astype(f32)
+            for m in range(1, 4):
+                total += CGZ[m].astype(f32)
+            CGF[d] = total.astype(bf16)
+            cgf_cp = [send(CGF.at[d], CGF.at[d], dpeer(k), t) for k in range(1, 4)]
+            grad_gather.pass_on(3)
         grad_gather.ready(n)
         cols = pl.ds(pl.multiple_of(1152 * p, 128), 1152)
         even, odd = RS[2 * p], RS[2 * p + 1]
@@ -550,9 +596,6 @@
         gn = mm(w_own, g, 1, 1)
         gain_sum += jnp.sum(gn * xhat, axis=1, keepdims=True)
         GF[:, cols] = stats[1:2] * (gn * go - stats[2:3] - xhat * stats[3:4])
-    for cp in turn_cp[0:7]:
-        cp.wait_recv()
-    ta_cp = [send(TA.at[0, d], TA.at[0, d], dpeer(k), t) for k in range(1, 4)]
     place_sum = jnp.zeros((128, 1152), f32)
     for p in range(4):
         cols = slice(1152 * p, 1152 * (p + 1))
@@ -578,13 +621,6 @@
         total += PR[n].astype(f32)
     PF[d] = total.astype(bf16)
     pf_cp = [send(PF.at[d], PF.at[d], dpeer(k), t) for k in range(1, 4)]
-    for cp in cgz_cp:
-        cp.wait_recv()
-    total = CGZ[0].astype(f32)
-    for m in range(1, 4):
-        total += CGZ[m].astype(f32)
-    CGF[d] = total.astype(bf16)
-    cgf_cp = [send(CGF.at[d], CGF.at[d], dpeer(k), t) for k in range(1, 4)]
     for cp in grf_cp:
         cp.wait_recv()
     for q in range(4):
@@ -613,7 +649,7 @@
 
 
 SCRATCH = (
-    ("readout_weight", (512, 1024), bf16), ("cotangent", (512, 1152), bf16), ("RO", (512, 1152), bf16), ("GF", (128, 4608), f32), ("SP", (128, 4608), f32), ("WT", (256, 256), bf16), ("WC", (256, 256), bf16), ("CB", (32, 3584), bf16),
+    ("features", (128, 4608), bf16), ("position", (576, 128), f32), ("conv_weight", (9, 32, 256), bf16), ("expand_weight", (32, 1024), bf16), ("readout_weight", (512, 1024), bf16), ("cotangent", (512, 1152), bf16), ("RO", (512, 1152), bf16), ("GF", (128, 4608), f32), ("SP", (128, 4608), f32), ("WT", (256, 256), bf16), ("WC", (256, 256), bf16), ("CB", (32, 3584), bf16),
     ("WQ", (4, 32, 896), bf16), ("WB", (2, 4, 4, 32, 896), bf16), ("WF", (256, 3584), bf16), ("MT", (512, 256), bf16),
     ("POOL", (288, 1152), bf16), ("PLC", (128, 4608), f32), ("XW", (2, 4, 128, 640), bf16), ("XK", (4, 256, 640), bf16),
     ("ST", (8, 4, 640), f32), ("SR", (8, 4, 640), f32), ("QF", (640, 256), f32), ("QS", (3, 576, 256), bf16),
@@ -690,10 +726,10 @@
         out_shape=shapes(
             ((512, 1152), bf16), ((128, 4608), f32), ((640, 128), f32), ((32, 1024), f32), ((32, 1024), f32), ((32, 2560), bf16), ((512, 1024), bf16)
         ),
-        in_specs=[vmem, smem] + [vmem] * 7 + [hbm] * 2,
+        in_specs=[hbm, smem, hbm, vmem, vmem, vmem, hbm, vmem, hbm, hbm, hbm],
         out_specs=[hbm, hbm, vmem, vmem, vmem, vmem, hbm],
         scratch_shapes=[pltpu.VMEM(shape, dtype) for _, shape, dtype in SCRATCH]
-        + [pltpu.SemaphoreType.DMA((COPIES,)), pltpu.SemaphoreType.DMA((COPIES,)), pltpu.SemaphoreType.DMA((16,))],
+        + [pltpu.SemaphoreType.DMA((COPIES,)), pltpu.SemaphoreType.DMA((COPIES,)), pltpu.SemaphoreType.DMA((24,))],
         compiler_params=pltpu.CompilerParams(collective_id=0, has_side_effects=True, vmem_limit_bytes=60 * 2**20),
     )(
         features, slot_live, position.reshape(576, 128), gain_outer.reshape(1, 128), reduce_weight.T, gain_middle.reshape(1, 32),

time: 143 us -> 138 us (0.965)
  Pallas kernels: 142 us -> 137 us
    pallas_call x1, Pallas kernels: 137 us -> 132 us  [local_by_image(): pl.pallas_call(kernel, out_shape=shapes(((512, 1152), bf16), ((128, 4608)...]
where the time goes in v5:
time: 138 us
  Pallas kernels  137 us (99%)
    pallas_call x1, Pallas kernels, local_by_image(): pl.pallas_call(kernel, out_shape=shapes(((512, 1152), bf16), ((128, 4608)...  132 us
    pallas_call x1, Pallas kernels, local_by_image(): pl.pallas_call(finish, out_shape=shapes(((512, 1152), bf16), ((128, 4608)...  5.04 us

profile of v5, /device:TPU:0, one launch (start us, length us, event | category | flops | bytes accessed | tf_op | source)
XLA Modules:
  0.0 138.3 jit_solution(13173582968219731109)
XLA Ops:
  0.6 132.4 %shard_map.186 = (bf16[512,1152]{1,0:T(8,128)(2,1)}, f32[128,4608]{1,0:T(8,128)}, f32[640,128]{1,0:T(8,128)}, f32[32,1024]{1,0:T(8,128)}, f32[32,1024]{1,0:T(8,1...) custom-call(bf16[128,4608]{1,0:T(8,128)(2,1)} %features_h.1, s32[8]{0:T(128)} %slot_live.1, ...), custom_call_target="tpu_custom_call" | custom-call | tf_op jit(solution)/shard_map/pallas_call | solution.py:724
  133.1 5.0 %shard_map.187 = (bf16[512,1152]{1,0:T(8,128)(2,1)}, f32[128,4608]{1,0:T(8,128)}, f32[576,128]{1,0:T(8,128)}, f32[1,128]{1,0:T(1,128)}, f32[32,1024]{1,0:T(8,128...) custom-call(bf16[512,1152]{1,0:T(8,128)(2,1)} %get-tuple-element.27., ...), custom_call_target="tpu_custom_call" | custom-call | tf_op jit(solution)/shard_map/pallas_call | solution.py:738

commit v6 on v5

--- a/solution.py
+++ b/solution.py
@@ -253,11 +253,6 @@
         x_cp.append(send(XW.at[1 - c, p], XK.at[p, pl.ds(pl.multiple_of(128 * c, 128), 128)], d, sib))
         XK[p, pl.ds(pl.multiple_of(128 * c, 128), 128), :] = XW[c, p]
 
-    for p in range(4):
-        high, low = split(PLC[:, 1152 * p : 1152 * (p + 1)])
-        PP[t, 288 * p : 288 * (p + 1), :] = (mm(POOL[...], high, 1, 1) + mm(POOL[...], low, 1, 1)).astype(bf16)
-    placed_gather = Gather(PP, 1)
-    placed_gather.start(far_mid)
     for cp in weight_cp:
         cp.wait()
     for n in range(9):
@@ -280,6 +275,10 @@
     WB[c, d, z] = quarter[...]
     wb_cp = [send(WQ.at[z], WB.at[c, d, z], dpeer(k), t) for k in range(1, 4)]
 
+    for p in range(4):
+        high, low = split(PLC[:, 1152 * p : 1152 * (p + 1)])
+        PP[t, 288 * p : 288 * (p + 1), :] = (mm(POOL[...], high, 1, 1) + mm(POOL[...], low, 1, 1)).astype(bf16)
+    placed_gather = Gather(PP, 1)
     for cp in w_cp:
         cp.wait_recv()
     WC[...] = mm(eye(256), WT[...], 1, 1).astype(bf16)
@@ -300,6 +299,7 @@
         if n == 0:
             st_cp = [send(ST.at[(t + k) % 8], SR.at[t], d, (t + k) % 8) for k in range(1, 8)]
             SR[t] = ST[t]
+    placed_gather.start(far_mid)
     placed_gather.start(partner)
     placed_gather.own()
 
@@ -486,8 +486,6 @@
     dyx_middle = dy * xm
     gr = norm_rows_back(dy * gm, xm, RM[:, 0:1]).reshape(24, 32, 256)[:, 0:24, :].reshape(576, 256).astype(bf16)
     GA[t] = gr
-    grad_gather = Gather(GA, 4)
-    grad_gather.start(far_mid)
     wg = jnp.sum(sums, axis=0, keepdims=True)
     grad_rounded = gr.astype(f32)
     s1 = jnp.sum(grad_rounded * wg, axis=1, keepdims=True)
@@ -501,6 +499,8 @@
     RS[t, 1:2, :] = rstd
     RS[t, 2:4, :] = row_sums[0:2]
     rs_cp = [send(RS.at[t], RS.at[t], d, (t + k) % 8) for k in range(1, 8)]
+    grad_gather = Gather(GA, 4)
+    grad_gather.start(far_mid)
     grad_gather.start(partner)
     pooled_sum.start(2)
     grad_gather.own()

time: 138 us -> 136 us (0.986)
  Pallas kernels: 137 us -> 135 us
    pallas_call x1, Pallas kernels: 132 us -> 130 us  [local_by_image(): pl.pallas_call(kernel, out_shape=shapes(((512, 1152), bf16), ((128, 4608)...]
where the time goes in v6:
time: 136 us
  Pallas kernels  135 us (99%)
    pallas_call x1, Pallas kernels, local_by_image(): pl.pallas_call(kernel, out_shape=shapes(((512, 1152), bf16), ((128, 4608)...  130 us
    pallas_call x1, Pallas kernels, local_by_image(): pl.pallas_call(finish, out_shape=shapes(((512, 1152), bf16), ((128, 4608)...  5.04 us

profile of v6, /device:TPU:0, one launch (start us, length us, event | category | flops | bytes accessed | tf_op | source)
XLA Modules:
  0.0 135.9 jit_solution(15593097190233552815)
XLA Ops:
  0.6 130.0 %shard_map.186 = (bf16[512,1152]{1,0:T(8,128)(2,1)}, f32[128,4608]{1,0:T(8,128)}, f32[640,128]{1,0:T(8,128)}, f32[32,1024]{1,0:T(8,128)}, f32[32,1024]{1,0:T(8,1...) custom-call(bf16[128,4608]{1,0:T(8,128)(2,1)} %features_h.1, s32[8]{0:T(128)} %slot_live.1, ...), custom_call_target="tpu_custom_call" | custom-call | tf_op jit(solution)/shard_map/pallas_call | solution.py:724
  130.7 5.0 %shard_map.187 = (bf16[512,1152]{1,0:T(8,128)(2,1)}, f32[128,4608]{1,0:T(8,128)}, f32[576,128]{1,0:T(8,128)}, f32[1,128]{1,0:T(1,128)}, f32[32,1024]{1,0:T(8,128...) custom-call(bf16[512,1152]{1,0:T(8,128)(2,1)} %get-tuple-element.27., ...), custom_call_target="tpu_custom_call" | custom-call | tf_op jit(solution)/shard_map/pallas_call | solution.py:738

commit v7 on v6

--- a/solution.py
+++ b/solution.py
@@ -311,13 +311,13 @@
         WB[c, d, block] = WQ[block]
     reduced_sum.add(0)
     placed_gather.forward(far_mid, 0)
-    reduced_sum.add(1)
     ws_cp = [send(WB.at[c, d], WB.at[c, d], d, sib)]
     for k in range(1, 4):
         for n in range(4):
             wb_cp[3 * n + k - 1].wait_recv()
         quarter = (d + 4 - k) % 4
         ws_cp.append(send(WB.at[c, quarter], WB.at[c, quarter], d, sib))
+    reduced_sum.add(1)
     for cp in ws_cp:
         cp.wait_recv()
 

time: 136 us -> 136 us (level)
  no operation moved by 1% of the time
where the time goes in v7:
time: 136 us
  Pallas kernels  135 us (99%)
    pallas_call x1, Pallas kernels, local_by_image(): pl.pallas_call(kernel, out_shape=shapes(((512, 1152), bf16), ((128, 4608)...  130 us
    pallas_call x1, Pallas kernels, local_by_image(): pl.pallas_call(finish, out_shape=shapes(((512, 1152), bf16), ((128, 4608)...  5.04 us

profile of v7, /device:TPU:0, one launch (start us, length us, event | category | flops | bytes accessed | tf_op | source)
XLA Modules:
  0.0 135.9 jit_solution(8892828437820622279)
XLA Ops:
  0.6 130.0 %shard_map.186 = (bf16[512,1152]{1,0:T(8,128)(2,1)}, f32[128,4608]{1,0:T(8,128)}, f32[640,128]{1,0:T(8,128)}, f32[32,1024]{1,0:T(8,128)}, f32[32,1024]{1,0:T(8,1...) custom-call(bf16[128,4608]{1,0:T(8,128)(2,1)} %features_h.1, s32[8]{0:T(128)} %slot_live.1, ...), custom_call_target="tpu_custom_call" | custom-call | tf_op jit(solution)/shard_map/pallas_call | solution.py:724
  130.7 5.0 %shard_map.187 = (bf16[512,1152]{1,0:T(8,128)(2,1)}, f32[128,4608]{1,0:T(8,128)}, f32[576,128]{1,0:T(8,128)}, f32[1,128]{1,0:T(1,128)}, f32[32,1024]{1,0:T(8,128...) custom-call(bf16[512,1152]{1,0:T(8,128)(2,1)} %get-tuple-element.27., ...), custom_call_target="tpu_custom_call" | custom-call | tf_op jit(solution)/shard_map/pallas_call | solution.py:738
